TPU v7x, 512 devices: a whole 4x4x16 slice. The times are simulated.
512 devices in a mesh: rows: 32 (over y, z_lo, core), cols: 16 (over z_hi, x).
Axes of the slice: x: 4, y: 4, z: 16 (z_hi: 4, z_lo: 4; z = z_hi * 4 + z_lo), core: 2. Of those that a mesh axis runs over, the one named last changes fastest.
Arguments:
- level_input: bfloat16 [64, 512, 2048], P(None, 'rows', 'cols'), may hold values from -6 to 6
- kernel_a: bfloat16 [64, 64, 3, 3], replicated, may hold values from -0.25 to 0.25
- kernel_b: bfloat16 [128, 64, 3, 3], replicated, may hold values from -0.25 to 0.25
- kernel_c: bfloat16 [64, 128, 3, 3], replicated, may hold values from -0.1875 to 0.1875
- kernel_d: bfloat16 [64, 64, 3, 3], replicated, may hold values from -0.25 to 0.25
- cotangent: bfloat16 [64, 512, 2048], P(None, 'rows', 'cols'), may hold values from -6 to 6
Outputs:
- result_field: bfloat16 [64, 512, 2048], P(None, 'rows', 'cols')
- input_grad: bfloat16 [64, 512, 2048], P(None, 'rows', 'cols')
- grad_a: float32 [64, 64, 3, 3], replicated
- grad_b: float32 [128, 64, 3, 3], replicated
- grad_c: float32 [64, 128, 3, 3], replicated
- grad_d: float32 [64, 64, 3, 3], replicated
All inputs are finite; a program needn't handle non-finite values.
Results may differ from a plain program's by a relative error of at most 0.017.
Values may be sent and summed in bfloat16 or wider, within the bound.
A program may use at most 64 MiB of HBM per device.

v0:
```python
import math

import jax
import jax.numpy as jnp
from jax import lax
from jax.sharding import PartitionSpec as P


def with_halo(array, sides, width):
    for axis, dim in sides:
        peers, length = (lax.axis_size(axis), array.shape[dim])
        up = [(i, (i + 1) % peers) for i in range(peers - 1)]
        down = [(j, i) for i, j in up]
        last = lax.slice_in_dim(array, length - width, length, axis=dim)
        initial = lax.slice_in_dim(array, 0, width, axis=dim)
        before = lax.ppermute(last, axis, up)
        after = lax.ppermute(initial, axis, down)
        array = jnp.concatenate([before, array, after], axis=dim)
    return array


def conv_valid(padded, kernel):
    result = lax.conv_general_dilated(
        padded[None],
        kernel,
        (1, 1),
        "VALID",
        dimension_numbers=("NCHW", "OIHW", "NCHW"),
        preferred_element_type=jnp.float32,
    )
    return result[0]


def kernel_grad(padded, upstream):
    height = upstream.shape[1]
    width_cells = upstream.shape[2]
    tap_list = []
    for shift_y in range(3):
        tap_row = []
        for shift_x in range(3):
            window = padded[:, shift_y : shift_y + height, shift_x : shift_x + width_cells]
            tap_row.append(
                lax.dot_general(
                    upstream,
                    window,
                    (((1, 2), (1, 2)), ((), ())),
                    preferred_element_type=jnp.float32,
                )
            )
        tap_list.append(jnp.stack(tap_row, axis=-1))
    return jnp.stack(tap_list, axis=-2)


def flipped(kernel):
    return jnp.transpose(kernel[:, :, ::-1, ::-1], (1, 0, 2, 3))


def block_view(field):
    channels, height, width_cells = field.shape
    return field.astype(jnp.float32).reshape(channels, height // 2, 2, width_cells // 2, 2)


def pooled(field):
    return jnp.mean(block_view(field), axis=(2, 4)).astype(jnp.bfloat16)


def block_sum(field):
    return jnp.sum(block_view(field), axis=(2, 4)).astype(jnp.bfloat16)


def upsampled(field):
    return jnp.repeat(jnp.repeat(field, 2, axis=1), 2, axis=2)


def gelu_back(preact, upstream):
    return jax.vjp(jax.nn.gelu, preact)[1](upstream)[0]


def fine_pad(field):
    return with_halo(field, (("rows", 1), ("cols", 2)), 1)


def coarse_pad(field):
    return with_halo(field, (("rows", 1), ("cols", 2)), 1)


def body(level_input, kernel_a, kernel_b, kernel_c, kernel_d, cotangent):
    padded_in = with_halo(level_input, (("rows", 1), ("cols", 2)), 1)
    padded_cot = None
    pre_a = conv_valid(padded_in, kernel_a)
    hidden = jax.nn.gelu(pre_a).astype(jnp.bfloat16)
    coarse = pooled(hidden)
    padded_coarse = coarse_pad(coarse)
    pre_b = conv_valid(padded_coarse, kernel_b)
    middle = jax.nn.gelu(pre_b).astype(jnp.bfloat16)
    padded_middle = coarse_pad(middle)
    coarse_out = conv_valid(padded_middle, kernel_c).astype(jnp.bfloat16)
    joined = (hidden.astype(jnp.float32) + upsampled(coarse_out).astype(jnp.float32)).astype(
        jnp.bfloat16
    )
    padded_joined = fine_pad(joined)
    result_field = conv_valid(padded_joined, kernel_d).astype(jnp.bfloat16)
    padded_cot = with_halo(cotangent, (("rows", 1), ("cols", 2)), 1)
    grad_joined = conv_valid(padded_cot, flipped(kernel_d)).astype(jnp.bfloat16)
    sum_d = kernel_grad(padded_joined, cotangent)
    grad_coarse = block_sum(grad_joined)
    sum_c = kernel_grad(padded_middle, grad_coarse)
    grad_pre_b = gelu_back(pre_b, conv_valid(coarse_pad(grad_coarse), flipped(kernel_c))).astype(
        jnp.bfloat16
    )
    sum_b = kernel_grad(padded_coarse, grad_pre_b)
    grad_pooled = conv_valid(coarse_pad(grad_pre_b), flipped(kernel_b)).astype(jnp.bfloat16)
    grad_hidden = grad_joined.astype(jnp.float32) + 0.25 * upsampled(grad_pooled).astype(
        jnp.float32
    )
    grad_pre_a = gelu_back(pre_a, grad_hidden).astype(jnp.bfloat16)
    input_grad = conv_valid(fine_pad(grad_pre_a), flipped(kernel_a)).astype(jnp.bfloat16)
    sum_a = kernel_grad(padded_in, grad_pre_a)
    sum_a, sum_b, sum_c, sum_d = lax.psum((sum_a, sum_b, sum_c, sum_d), ("rows", "cols"))
    total_cells = (
        level_input.shape[1] * level_input.shape[2] * lax.axis_size("rows") * lax.axis_size("cols")
    )
    fine_scale = 1.0 / math.sqrt(total_cells)
    coarse_scale = 1.0 / math.sqrt(total_cells // 4)
    return (
        result_field,
        input_grad,
        sum_a * fine_scale,
        sum_b * coarse_scale,
        sum_c * coarse_scale,
        sum_d * fine_scale,
    )


def solution(mesh):
    placed = (P(None, "rows", "cols"), P(), P(), P(), P(), P(None, "rows", "cols"))
    return jax.shard_map(
        body,
        mesh=mesh,
        in_specs=placed,
        out_specs=(P(None, "rows", "cols"), P(None, "rows", "cols"), P(), P(), P(), P()),
        check_vma=False,
    )
```

profile of v0, /device:TPU:1, one launch (start us, length us, event | category | flops | bytes accessed | tf_op | source)
XLA Modules:
  0.0 772.1 jit_solution(8292148814598889432)
XLA Ops:
  8.3 4.9 collective-permute-start.16
  13.2 5.1 collective-permute-start.17
  21.4 3.8 collective-permute-start
  30.8 4.0 collective-permute-start.2
  37.4 4.1 collective-permute-done.19
  47.5 4.3 collective-permute-start.20
  51.8 1.9 collective-permute-start.21
  58.8 3.6 collective-permute-start.4
  67.7 8.3 %collective-permute-start.6 = (bf16[64,10,1]{2,0,1:T(8,128)(2,1)S(1)}, bf16[64,10,1]{2,0,1:T(8,128)(2,1)S(1)}, u32[]{:S(2)}, u32[]{:S(2)}) collective-permute-start(bf16[64,10,1]{2,0,1:T(8,128)(2,1)S(1)} %get-tuple-element.60), channel_id=1, source_target_pairs={{0,1},{1,2},{2,3},{3,4},{4,5},{5,6},{6,7},{7,8},{8,9},{9,10},{10,1... | collective-permute-start | bytes 3848 | tf_op jit(solution)/shard_map/ppermute | solution.py:16
  78.9 52.6 %collective-permute-done.7 = bf16[64,10,1]{2,0,1:T(8,128)(2,1)S(1)} collective-permute-done((bf16[64,10,1]{2,0,1:T(8,128)(2,1)S(1)}, bf16[64,10,1]{2,0,1:T(8,128)(2,1)S(1)}, u32[]{:S(2)}, u32[]{:S(2)}) %collective-permute-start.7) | collective-permute-done | bytes 1312 | tf_op jit(solution)/shard_map/ppermute | solution.py:17
  134.9 4.0 collective-permute-start.8
  140.8 3.6 collective-permute-start.24
  147.6 3.6 collective-permute-start.10
  152.6 8.3 %collective-permute-start.26 = (bf16[128,10,1]{0,2,1:T(2,128)(2,1)S(1)}, bf16[128,10,1]{0,2,1:T(2,128)(2,1)S(1)}, u32[]{:S(2)}, u32[]{:S(2)}) collective-permute-start(bf16[128,10,1]{0,2,1:T(2,128)(2,1)S(1)} %get-tuple-element.54), channel_id=1, source_target_pairs={{0,1},{1,2},{2,3},{3,4},{4,5},{5,6},{6,7},{7,8},{8,9},{9,10},{10,1... | collective-permute-start | bytes 7688 | tf_op jit(solution)/shard_map/ppermute | solution.py:16
  168.3 8.6 %collective-permute-done.27 = bf16[128,10,1]{0,2,1:T(2,128)(2,1)S(1)} collective-permute-done((bf16[128,10,1]{0,2,1:T(2,128)(2,1)S(1)}, bf16[128,10,1]{0,2,1:T(2,128)(2,1)S(1)}, u32[]{:S(2)}, u32[]{:S(2)}) %collective-permute-start.27) | collective-permute-done | bytes 2592 | tf_op jit(solution)/shard_map/ppermute | solution.py:17
  183.0 5.1 collective-permute-start.12
  188.1 1.9 collective-permute-start.13
  190.0 3.6 collective-permute-start.28
  193.7 1.9 collective-permute-start.29
  200.8 6.1 collective-permute-start.30
  208.3 5.8 collective-permute-start.14
  216.0 3.0 collective-permute-done.14
  219.1 10.1 %collective-permute-done.15 = bf16[64,18,1]{2,0,1:T(8,128)(2,1)S(1)} collective-permute-done((bf16[64,18,1]{2,0,1:T(8,128)(2,1)S(1)}, bf16[64,18,1]{2,0,1:T(8,128)(2,1)S(1)}, u32[]{:S(2)}, u32[]{:S(2)}) %collective-permute-start.15) | collective-permute-done | bytes 2336 | tf_op jit(solution)/shard_map/ppermute | solution.py:17
  240.3 520.0 %all-reduce.3.cloned.1.call-done = (f32[64,64,3,3]{1,0,3,2:T(8,128)}, f32[128,64,3,3]{0,1,3,2:T(8,128)}, f32[64,128,3,3]{1,0,3,2:T(8,128)}, f32[64,64,3,3]{1,0,3,2:T(8,128)}) async-done(((f32[64,64,3,3]{1,0,3,2:T(8,128)}, f32[128,64,3,3]{0,1,3,2:T(8,128)}, f32[64,128,3,3]{1,0,3,2:T(8,128)}, f32[64,64,3,3]{1,0,3,2:T(8,128)}), (f32[64,64,3,3]{1,0,3,2:T(8,128)}, f32[128,64,3,3]{0,1,3,2:T(8,128)}, ...) | async-done | bytes 884752 | tf_op jit(solution)/shard_map/psum | solution.py:119
  (271 shorter events, 77.9 us)
Async XLA Ops:
  7.2 753.2 %all-reduce.3.cloned.1.call-start = ((), (), s32[]{:S(2)}) async-start(), calls=%async_computation | async-start | bytes 2359296 | tf_op jit(solution)/shard_map/psum | solution.py:119
  8.3 16.9 %collective-permute-start.16 = (bf16[64,1,128]{2,1,0:T(2,128)(2,1)S(1)}, bf16[64,1,128]{2,1,0:T(2,128)(2,1)S(1)}, u32[]{:S(2)}, u32[]{:S(2)}) collective-permute-start(bf16[64,1,128]{2,1,0:T(2,128)(2,1)S(1)} %get-tuple-element.44), channel_id=1, source_target_pairs={{0,16},{16,32},{32,48},{48,64},{64,80},{80,96},{96,112},{112,128},... | collective-permute-start | bytes 49160 | tf_op jit(solution)/shard_map/ppermute | solution.py:16
  13.2 11.9 %collective-permute-start.17 = (bf16[64,1,128]{2,1,0:T(2,128)(2,1)S(1)}, bf16[64,1,128]{2,1,0:T(2,128)(2,1)S(1)}, u32[]{:S(2)}, u32[]{:S(2)}) collective-permute-start(bf16[64,1,128]{2,1,0:T(2,128)(2,1)S(1)} %get-tuple-element.45), channel_id=1, source_target_pairs={{16,0},{32,16},{48,32},{64,48},{80,64},{96,80},{112,96},{128,112},... | collective-permute-start | bytes 49160 | tf_op jit(solution)/shard_map/ppermute | solution.py:17
  28.5 13.0 %collective-permute-start.19 = (bf16[64,18,1]{2,1,0:T(8,128)(2,1)S(1)}, bf16[64,18,1]{2,1,0:T(8,128)(2,1)S(1)}, u32[]{:S(2)}, u32[]{:S(2)}) collective-permute-start(bf16[64,18,1]{2,1,0:T(8,128)(2,1)S(1)} %get-tuple-element.31), channel_id=1, source_target_pairs={{1,0},{2,1},{3,2},{4,3},{5,4},{6,5},{7,6},{8,7},{9,8},{10,9},{11,1... | collective-permute-start | bytes 6920 | tf_op jit(solution)/shard_map/ppermute | solution.py:17
  30.8 23.0 %collective-permute-start.2 = (bf16[64,18,1]{2,0,1:T(8,128)(2,1)}, bf16[64,18,1]{2,0,1:T(8,128)(2,1)S(1)}, u32[]{:S(2)}, u32[]{:S(2)}) collective-permute-start(bf16[64,18,1]{2,0,1:T(8,128)(2,1)} %get-tuple-element.38), channel_id=1, source_target_pairs={{0,1},{1,2},{2,3},{3,4},{4,5},{5,6},{6,7},{7,8},{8,9},{9,10},{10,1... | collective-permute-start | bytes 6920 | tf_op jit(solution)/shard_map/ppermute | solution.py:16
  34.8 19.0 %collective-permute-start.3 = (bf16[64,18,1]{2,0,1:T(8,128)(2,1)}, bf16[64,18,1]{2,0,1:T(8,128)(2,1)S(1)}, u32[]{:S(2)}, u32[]{:S(2)}) collective-permute-start(bf16[64,18,1]{2,0,1:T(8,128)(2,1)} %get-tuple-element.39), channel_id=1, source_target_pairs={{1,0},{2,1},{3,2},{4,3},{5,4},{6,5},{7,6},{8,7},{9,8},{10,9},{11,1... | collective-permute-start | bytes 6920 | tf_op jit(solution)/shard_map/ppermute | solution.py:17
  47.5 16.9 %collective-permute-start.20 = (bf16[64,1,64]{0,2,1:T(8,128)(2,1)S(1)}, bf16[64,1,64]{0,2,1:T(8,128)(2,1)S(1)}, u32[]{:S(2)}, u32[]{:S(2)}) collective-permute-start(bf16[64,1,64]{0,2,1:T(8,128)(2,1)S(1)} %get-tuple-element.64), channel_id=1, source_target_pairs={{0,16},{16,32},{32,48},{48,64},{64,80},{80,96},{96,112},{112,128},... | collective-permute-start | bytes 24584 | tf_op jit(solution)/shard_map/ppermute | solution.py:16
  51.8 12.6 %collective-permute-start.21 = (bf16[64,1,64]{0,2,1:T(8,128)(2,1)S(1)}, bf16[64,1,64]{0,2,1:T(8,128)(2,1)S(1)}, u32[]{:S(2)}, u32[]{:S(2)}) collective-permute-start(bf16[64,1,64]{0,2,1:T(8,128)(2,1)S(1)} %get-tuple-element.65), channel_id=1, source_target_pairs={{16,0},{32,16},{48,32},{64,48},{80,64},{96,80},{112,96},{128,112},... | collective-permute-start | bytes 24584 | tf_op jit(solution)/shard_map/ppermute | solution.py:17
  64.4 13.1 %collective-permute-start.22 = (bf16[64,10,1]{0,2,1:T(2,128)(2,1)S(1)}, bf16[64,10,1]{0,2,1:T(2,128)(2,1)S(1)}, u32[]{:S(2)}, u32[]{:S(2)}) collective-permute-start(bf16[64,10,1]{0,2,1:T(2,128)(2,1)S(1)} %get-tuple-element.56), channel_id=1, source_target_pairs={{0,1},{1,2},{2,3},{3,4},{4,5},{5,6},{6,7},{7,8},{8,9},{9,10},{10,1... | collective-permute-start | bytes 3848 | tf_op jit(solution)/shard_map/ppermute | solution.py:16
  65.7 11.8 %collective-permute-start.23 = (bf16[64,10,1]{0,2,1:T(2,128)(2,1)S(1)}, bf16[64,10,1]{0,2,1:T(2,128)(2,1)S(1)}, u32[]{:S(2)}, u32[]{:S(2)}) collective-permute-start(bf16[64,10,1]{0,2,1:T(2,128)(2,1)S(1)} %get-tuple-element.57), channel_id=1, source_target_pairs={{1,0},{2,1},{3,2},{4,3},{5,4},{6,5},{7,6},{8,7},{9,8},{10,9},{11,1... | collective-permute-start | bytes 3848 | tf_op jit(solution)/shard_map/ppermute | solution.py:17
  67.7 11.1 %collective-permute-start.6 = (bf16[64,10,1]{2,0,1:T(8,128)(2,1)S(1)}, bf16[64,10,1]{2,0,1:T(8,128)(2,1)S(1)}, u32[]{:S(2)}, u32[]{:S(2)}) collective-permute-start(bf16[64,10,1]{2,0,1:T(8,128)(2,1)S(1)} %get-tuple-element.60), channel_id=1, source_target_pairs={{0,1},{1,2},{2,3},{3,4},{4,5},{5,6},{6,7},{7,8},{8,9},{9,10},{10,1... | collective-permute-start | bytes 3848 | tf_op jit(solution)/shard_map/ppermute | solution.py:16
  76.0 55.5 %collective-permute-start.7 = (bf16[64,10,1]{2,0,1:T(8,128)(2,1)S(1)}, bf16[64,10,1]{2,0,1:T(8,128)(2,1)S(1)}, u32[]{:S(2)}, u32[]{:S(2)}) collective-permute-start(bf16[64,10,1]{2,0,1:T(8,128)(2,1)S(1)} %get-tuple-element.61), channel_id=1, source_target_pairs={{1,0},{2,1},{3,2},{4,3},{5,4},{6,5},{7,6},{8,7},{9,8},{10,9},{11,1... | collective-permute-start | bytes 3848 | tf_op jit(solution)/shard_map/ppermute | solution.py:17
  134.9 12.7 %collective-permute-start.8 = (bf16[128,1,64]{0,2,1:T(8,128)(2,1)S(1)}, bf16[128,1,64]{0,2,1:T(8,128)(2,1)S(1)}, u32[]{:S(2)}, u32[]{:S(2)}) collective-permute-start(bf16[128,1,64]{0,2,1:T(8,128)(2,1)S(1)} %get-tuple-element.66), channel_id=1, source_target_pairs={{0,16},{16,32},{32,48},{48,64},{64,80},{80,96},{96,112},{112,128},... | collective-permute-start | bytes 49160 | tf_op jit(solution)/shard_map/ppermute | solution.py:16
  140.8 11.8 %collective-permute-start.24 = (bf16[128,1,64]{0,2,1:T(8,128)(2,1)S(1)}, bf16[128,1,64]{0,2,1:T(8,128)(2,1)S(1)}, u32[]{:S(2)}, u32[]{:S(2)}) collective-permute-start(bf16[128,1,64]{0,2,1:T(8,128)(2,1)S(1)} %get-tuple-element.62), channel_id=1, source_target_pairs={{0,16},{16,32},{32,48},{48,64},{64,80},{80,96},{96,112},{112,128},... | collective-permute-start | bytes 49160 | tf_op jit(solution)/shard_map/ppermute | solution.py:16
  147.6 16.2 %collective-permute-start.10 = (bf16[128,10,1]{0,2,1:T(2,128)(2,1)S(1)}, bf16[128,10,1]{0,2,1:T(2,128)(2,1)S(1)}, u32[]{:S(2)}, u32[]{:S(2)}) collective-permute-start(bf16[128,10,1]{0,2,1:T(2,128)(2,1)S(1)} %get-tuple-element.58), channel_id=1, source_target_pairs={{0,1},{1,2},{2,3},{3,4},{4,5},{5,6},{6,7},{7,8},{8,9},{9,10},{10,1... | collective-permute-start | bytes 7688 | tf_op jit(solution)/shard_map/ppermute | solution.py:16
  151.3 12.6 %collective-permute-start.11 = (bf16[128,10,1]{0,2,1:T(2,128)(2,1)S(1)}, bf16[128,10,1]{0,2,1:T(2,128)(2,1)S(1)}, u32[]{:S(2)}, u32[]{:S(2)}) collective-permute-start(bf16[128,10,1]{0,2,1:T(2,128)(2,1)S(1)} %get-tuple-element.59), channel_id=1, source_target_pairs={{1,0},{2,1},{3,2},{4,3},{5,4},{6,5},{7,6},{8,7},{9,8},{10,9},{11,1... | collective-permute-start | bytes 7688 | tf_op jit(solution)/shard_map/ppermute | solution.py:17
  152.6 15.6 %collective-permute-start.26 = (bf16[128,10,1]{0,2,1:T(2,128)(2,1)S(1)}, bf16[128,10,1]{0,2,1:T(2,128)(2,1)S(1)}, u32[]{:S(2)}, u32[]{:S(2)}) collective-permute-start(bf16[128,10,1]{0,2,1:T(2,128)(2,1)S(1)} %get-tuple-element.54), channel_id=1, source_target_pairs={{0,1},{1,2},{2,3},{3,4},{4,5},{5,6},{6,7},{7,8},{8,9},{9,10},{10,1... | collective-permute-start | bytes 7688 | tf_op jit(solution)/shard_map/ppermute | solution.py:16
  160.9 16.0 %collective-permute-start.27 = (bf16[128,10,1]{0,2,1:T(2,128)(2,1)S(1)}, bf16[128,10,1]{0,2,1:T(2,128)(2,1)S(1)}, u32[]{:S(2)}, u32[]{:S(2)}) collective-permute-start(bf16[128,10,1]{0,2,1:T(2,128)(2,1)S(1)} %get-tuple-element.55), channel_id=1, source_target_pairs={{1,0},{2,1},{3,2},{4,3},{5,4},{6,5},{7,6},{8,7},{9,8},{10,9},{11,1... | collective-permute-start | bytes 7688 | tf_op jit(solution)/shard_map/ppermute | solution.py:17
  183.0 16.7 %collective-permute-start.12 = (bf16[64,1,128]{2,0,1:T(8,128)(2,1)S(1)}, bf16[64,1,128]{2,0,1:T(8,128)(2,1)S(1)}, u32[]{:S(2)}, u32[]{:S(2)}) collective-permute-start(bf16[64,1,128]{2,0,1:T(8,128)(2,1)S(1)} %get-tuple-element.46), channel_id=1, source_target_pairs={{0,16},{16,32},{32,48},{48,64},{64,80},{80,96},{96,112},{112,128},... | collective-permute-start | bytes 49160 | tf_op jit(solution)/shard_map/ppermute | solution.py:16
  188.1 11.6 %collective-permute-start.13 = (bf16[64,1,128]{2,0,1:T(8,128)(2,1)S(1)}, bf16[64,1,128]{2,0,1:T(8,128)(2,1)S(1)}, u32[]{:S(2)}, u32[]{:S(2)}) collective-permute-start(bf16[64,1,128]{2,0,1:T(8,128)(2,1)S(1)} %get-tuple-element.47), channel_id=1, source_target_pairs={{16,0},{32,16},{48,32},{64,48},{80,64},{96,80},{112,96},{128,112},... | collective-permute-start | bytes 49160 | tf_op jit(solution)/shard_map/ppermute | solution.py:17
  200.8 30.3 %collective-permute-start.30 = (bf16[64,18,1]{2,0,1:T(8,128)(2,1)S(1)}, bf16[64,18,1]{2,0,1:T(8,128)(2,1)S(1)}, u32[]{:S(2)}, u32[]{:S(2)}) collective-permute-start(bf16[64,18,1]{2,0,1:T(8,128)(2,1)S(1)} %get-tuple-element.34), channel_id=1, source_target_pairs={{0,1},{1,2},{2,3},{3,4},{4,5},{5,6},{6,7},{7,8},{8,9},{9,10},{10,1... | collective-permute-start | bytes 6920 | tf_op jit(solution)/shard_map/ppermute | solution.py:16
  207.0 24.2 %collective-permute-start.31 = (bf16[64,18,1]{2,0,1:T(8,128)(2,1)S(1)}, bf16[64,18,1]{2,0,1:T(8,128)(2,1)S(1)}, u32[]{:S(2)}, u32[]{:S(2)}) collective-permute-start(bf16[64,18,1]{2,0,1:T(8,128)(2,1)S(1)} %get-tuple-element.35), channel_id=1, source_target_pairs={{1,0},{2,1},{3,2},{4,3},{5,4},{6,5},{7,6},{8,7},{9,8},{10,9},{11,1... | collective-permute-start | bytes 6920 | tf_op jit(solution)/shard_map/ppermute | solution.py:17
  208.3 10.8 %collective-permute-start.14 = (bf16[64,18,1]{2,0,1:T(8,128)(2,1)S(1)}, bf16[64,18,1]{2,0,1:T(8,128)(2,1)S(1)}, u32[]{:S(2)}, u32[]{:S(2)}) collective-permute-start(bf16[64,18,1]{2,0,1:T(8,128)(2,1)S(1)} %get-tuple-element.36), channel_id=1, source_target_pairs={{0,1},{1,2},{2,3},{3,4},{4,5},{5,6},{6,7},{7,8},{8,9},{9,10},{10,1... | collective-permute-start | bytes 6920 | tf_op jit(solution)/shard_map/ppermute | solution.py:16
  214.1 15.1 %collective-permute-start.15 = (bf16[64,18,1]{2,0,1:T(8,128)(2,1)S(1)}, bf16[64,18,1]{2,0,1:T(8,128)(2,1)S(1)}, u32[]{:S(2)}, u32[]{:S(2)}) collective-permute-start(bf16[64,18,1]{2,0,1:T(8,128)(2,1)S(1)} %get-tuple-element.37), channel_id=1, source_target_pairs={{1,0},{2,1},{3,2},{4,3},{5,4},{6,5},{7,6},{8,7},{9,8},{10,9},{11,1... | collective-permute-start | bytes 6920 | tf_op jit(solution)/shard_map/ppermute | solution.py:17
  (40 other events, 386.1 us)
Sparse Core Ops, SparseCore 0:
  237.5 522.8 all-reduce.2
where the time goes:
time: 774 us; the launch traced here: 772 us
  waiting for transfers between devices  602 us (78%)
  starting transfers between devices  101 us (13%)
  matrix products  19.6 us (3%)
  local copies, waits for them, and re-layouts  18.4 us (2%)
  other arithmetic  15.7 us (2%)
  between operations  15.7 us (2%)
    psum x1, waiting for transfers between devices, body(): lax.psum((sum_a, sum_b, sum_c, sum_d), ('rows', 'cols'))  520 us
    ppermute x16, waiting for transfers between devices, with_halo(): after = lax.ppermute(initial, axis, down)  76.7 us
    ppermute x16, starting transfers between devices, with_halo(): before = lax.ppermute(last, axis, up)  71.7 us
    ppermute x16, starting transfers between devices, with_halo(): after = lax.ppermute(initial, axis, down)  29.3 us
  transfers between devices with their start and end apart: 33, of which 10 were waited for; matrix products, arithmetic and copies ran while one was open for 4% of the time, Pallas kernels for 0%

commit v1 on v0

--- a/solution.py
+++ b/solution.py
@@ -3,7 +3,147 @@
 import jax
 import jax.numpy as jnp
 from jax import lax
+from jax.experimental import pallas as pl
+from jax.experimental.pallas import tpu as pltpu
 from jax.sharding import PartitionSpec as P
+
+
+MESH = pl.DeviceIdType.MESH
+
+
+def _reduce_kernel(x_ref, out_ref, pair_out, pair_in, plane_out, plane_in, own, near_in, far, whole,
+                   pair_s, pair_r, plane_s, plane_r, near_s, near_r, far_s, far_r,
+                   gnear_s, gnear_r, gplane_s, gplane_r, gpair_s, gpair_r):
+    rows, cols = lax.axis_index("rows"), lax.axis_index("cols")
+    y, near, core = rows // 8, (rows // 2) % 4, rows % 2
+    far_at, x = cols // 4, cols % 4
+
+    def place(y_at, near_at, core_at, z_at, x_at):
+        return (y_at * 8 + near_at * 2 + core_at, z_at * 4 + x_at)
+
+    partner = place(y, near, 1 - core, far_at, x)
+
+    def plane_peer(dy, dx):
+        return place((y + dy) % 4, near, core, far_at, (x + dx) % 4)
+
+    def near_peer(dz):
+        return place(y, (near + dz) % 4, core, far_at, x)
+
+    def far_peer(dz):
+        return place(y, near, core, (far_at + dz) % 4, x)
+
+    plane_steps = [(dy, dx) for dy in (2, 1, 3, 0) for dx in (2, 1, 3, 0)]
+    barrier = pltpu.get_barrier_semaphore()
+    greeted = [partner]
+    greeted += [plane_peer(dy, dx) for dy, dx in plane_steps if (dy, dx) != (0, 0)]
+    greeted += [near_peer(dz) for dz in (1, 2, 3)] + [far_peer(dz) for dz in (1, 2, 3)]
+    for peer in greeted:
+        pl.semaphore_signal(barrier, inc=1, device_id=peer, device_id_type=MESH)
+
+    def send(src, dst, send_sem, recv_sem, peer):
+        copy = pltpu.make_async_remote_copy(
+            src_ref=src, dst_ref=dst, send_sem=send_sem, recv_sem=recv_sem,
+            device_id=peer, device_id_type=MESH)
+        copy.start()
+        return copy
+
+    theirs, mine = (1 - core) * 64, core * 64
+    started = []
+    for dy in (2, 1, 3, 0):
+        first = ((y + dy) % 4) * 16
+        pair_out[pl.ds(first, 16)] = x_ref[pl.ds(theirs + first, 16)].astype(jnp.bfloat16)
+    pl.semaphore_wait(barrier, len(greeted))
+    pair = {}
+    for dy in (2, 1, 3, 0):
+        piece = pl.ds(((y + dy) % 4) * 16, 16)
+        pair[dy] = send(pair_out.at[piece], pair_in.at[piece], pair_s.at[dy], pair_r.at[dy], partner)
+    plane = {}
+    for dy, dx in plane_steps:
+        if dx == 2:
+            pair[dy].wait_recv()
+        first = ((y + dy) % 4) * 16 + ((x + dx) % 4) * 4
+        chunk = pl.ds(first, 4)
+        both = x_ref[pl.ds(mine + first, 4)] + pair_in[chunk].astype(jnp.float32)
+        if (dy, dx) == (0, 0):
+            own[...] = both
+        else:
+            k = dy * 4 + dx
+            plane_out[chunk] = both.astype(jnp.bfloat16)
+            plane[k] = send(plane_out.at[chunk], plane_in.at[k], plane_s.at[k], plane_r.at[k],
+                            plane_peer(dy, dx))
+    total = own[...]
+    for k in (4, 12, 1, 3, 8, 2, 5, 7, 13, 15, 6, 14, 9, 11, 10):
+        plane[k].wait_recv()
+        total = total + plane_in[k].astype(jnp.float32)
+    own[...] = total
+    near_copies = {}
+    for dz in (2, 1, 3):
+        near_copies[dz] = send(own.at[(near + dz) % 4], near_in.at[dz], near_s.at[dz],
+                               near_r.at[dz], near_peer(dz))
+    tile = own[near]
+    for dz in (1, 3, 2):
+        near_copies[dz].wait_recv()
+        tile = tile + near_in[dz]
+    far[far_at] = tile
+    far_copies = {}
+    for dz in (2, 1, 3):
+        far_copies[dz] = send(far.at[far_at], far.at[far_at], far_s.at[dz], far_r.at[dz], far_peer(dz))
+    for dz in (1, 3, 2):
+        far_copies[dz].wait_recv()
+    tile = ((far[0] + far[1]) + far[2]) + far[3]
+    base = mine + y * 16 + x * 4
+    whole[base + near] = tile.astype(jnp.bfloat16)
+    gather = []
+    for dz in (2, 1, 3):
+        at = whole.at[base + near]
+        gather.append(send(at, at, gnear_s.at[dz], gnear_r.at[dz], near_peer(dz)))
+    for copy in gather:
+        copy.wait_recv()
+    gplane = {}
+    for dy, dx in plane_steps:
+        if (dy, dx) != (0, 0):
+            k = dy * 4 + dx
+            at = whole.at[pl.ds(base, 4)]
+            gplane[k] = send(at, at, gplane_s.at[k], gplane_r.at[k], plane_peer(dy, dx))
+    gpair = []
+    for dy in (0, 1, 3, 2):
+        for dx in (0, 1, 3, 2):
+            if (dy, dx) != (0, 0):
+                gplane[dy * 4 + dx].wait_recv()
+        at = whole.at[pl.ds(mine + ((y - dy + 4) % 4) * 16, 16)]
+        gpair.append(send(at, at, gpair_s.at[dy], gpair_r.at[dy], partner))
+    for copy in gpair:
+        copy.wait_recv()
+    out_ref[...] = whole[...].astype(jnp.float32)
+    for copies in (pair.values(), plane.values(), near_copies.values(), far_copies.values(), gather,
+                   gplane.values(), gpair):
+        for copy in copies:
+            copy.wait_send()
+
+
+def reduce_all(tiles):
+    dma = pltpu.SemaphoreType.DMA
+    return pl.pallas_call(
+        _reduce_kernel,
+        out_shape=jax.ShapeDtypeStruct((128, 16, 128), jnp.float32),
+        in_specs=[pl.BlockSpec(memory_space=pltpu.VMEM)],
+        out_specs=pl.BlockSpec(memory_space=pltpu.VMEM),
+        scratch_shapes=[
+            pltpu.VMEM((64, 16, 128), jnp.bfloat16),
+            pltpu.VMEM((64, 16, 128), jnp.bfloat16),
+            pltpu.VMEM((64, 16, 128), jnp.bfloat16),
+            pltpu.VMEM((16, 4, 16, 128), jnp.bfloat16),
+            pltpu.VMEM((4, 16, 128), jnp.float32),
+            pltpu.VMEM((4, 16, 128), jnp.float32),
+            pltpu.VMEM((4, 16, 128), jnp.float32),
+            pltpu.VMEM((128, 16, 128), jnp.bfloat16),
+            dma((4,)), dma((4,)), dma((16,)), dma((16,)), dma((4,)), dma((4,)), dma((4,)), dma((4,)),
+            dma((4,)), dma((4,)), dma((16,)), dma((16,)), dma((4,)), dma((4,)),
+        ],
+        compiler_params=pltpu.CompilerParams(
+            collective_id=1, has_side_effects=True, vmem_limit_bytes=32 * 1024 * 1024),
+        cost_estimate=pl.CostEstimate(flops=1000000, bytes_accessed=4000000, transcendentals=0),
+    )(tiles)
 
 
 def with_halo(array, sides, width):
@@ -116,7 +256,14 @@
     grad_pre_a = gelu_back(pre_a, grad_hidden).astype(jnp.bfloat16)
     input_grad = conv_valid(fine_pad(grad_pre_a), flipped(kernel_a)).astype(jnp.bfloat16)
     sum_a = kernel_grad(padded_in, grad_pre_a)
-    sum_a, sum_b, sum_c, sum_d = lax.psum((sum_a, sum_b, sum_c, sum_d), ("rows", "cols"))
+    sums = (sum_a, sum_b, sum_c, sum_d)
+    flat = jnp.concatenate([s.reshape(-1, 128) for s in sums] + [jnp.zeros((320, 128), jnp.float32)])
+    flat = reduce_all(flat.reshape(128, 16, 128)).reshape(2048, 128)
+    start, totals = 0, []
+    for s in sums:
+        totals.append(flat[start : start + s.size // 128].reshape(s.shape))
+        start += s.size // 128
+    sum_a, sum_b, sum_c, sum_d = totals
     total_cells = (
         level_input.shape[1] * level_input.shape[2] * lax.axis_size("rows") * lax.axis_size("cols")
     )

time: 774 us -> 512 us (0.66)
  waiting for transfers between devices: 602 us -> 61.3 us
  local copies, waits for them, and re-layouts: 18.4 us -> 174 us
  Pallas kernels: 0 us -> 109 us
  matrix products: 19.6 us -> 36.8 us
  between operations: 15.7 us -> 2.45 us
    psum x1 -> x0, waiting for transfers between devices: 520 us -> none  [body(): lax.psum((sum_a, sum_b, sum_c, sum_d), ('rows', 'cols'))]
    pallas_call x0 -> x1, Pallas kernels: none -> 109 us  [reduce_all(): pl.pallas_call(_reduce_kernel, out_shape=jax.ShapeDtypeStruct((128, 16, 1...]
    reshape x0 -> x4, local copies, waits for them, and re-layouts: none -> 42.2 us  [body(): s.reshape(-1, 128)]
    another operation x0 -> x4, local copies, waits for them, and re-layouts: none -> 36.6 us  [kernel_grad(): return jnp.stack(tap_list, axis=-2)]
    unnamed x74 -> x85, local copies, waits for them, and re-layouts: 8.85 us -> 43.7 us
    mul x0 -> x4, local copies, waits for them, and re-layouts: none -> 33.9 us  [the longest x1 10.9 us: body(): sum_c * coarse_scale]
    ppermute x16, waiting for transfers between devices: 76.7 us -> 53.5 us  [with_halo(): after = lax.ppermute(initial, axis, down)]
    conv_general_dilated x8, matrix products: 6.59 us -> 20 us  [conv_valid(): lax.conv_general_dilated(padded[None], kernel, (1, 1), 'VALID', dimension...]
  transfers between devices with their start and end apart: 33 -> 32, of which waited for: 10 -> 5; matrix products, arithmetic and copies ran while one was open for 4% -> 22% of each run, Pallas kernels for 0% -> 22%
where the time goes in v1:
time: 512 us; the launch traced here: 504 us
  local copies, waits for them, and re-layouts  174 us (34%)
  Pallas kernels  109 us (21%)
  starting transfers between devices  108 us (21%)
  waiting for transfers between devices  61.3 us (12%)
  matrix products  36.8 us (7%)
  other arithmetic  12.2 us (2%)
    pallas_call x1, Pallas kernels, reduce_all(): pl.pallas_call(_reduce_kernel, out_shape=jax.ShapeDtypeStruct((128, 16, 1...  109 us
    ppermute x16, starting transfers between devices, with_halo(): before = lax.ppermute(last, axis, up)  77.9 us
    ppermute x16, waiting for transfers between devices, with_halo(): after = lax.ppermute(initial, axis, down)  53.5 us
    unnamed x85, local copies, waits for them, and re-layouts  43.7 us
    reshape x4, local copies, waits for them, and re-layouts, body(): s.reshape(-1, 128)  42.2 us
    another operation x4, local copies, waits for them, and re-layouts, kernel_grad(): return jnp.stack(tap_list, axis=-2)  36.6 us
    ppermute x16, starting transfers between devices, with_halo(): after = lax.ppermute(initial, axis, down)  29.8 us
    conv_general_dilated x8, matrix products, conv_valid(): lax.conv_general_dilated(padded[None], kernel, (1, 1), 'VALID', dimension...  20 us
  transfers between devices with their start and end apart: 32, of which 5 were waited for; matrix products, arithmetic and copies ran while one was open for 22% of the time, Pallas kernels for 22%

profile of v1, /device:TPU:1, one launch (start us, length us, event | category | flops | bytes accessed | tf_op | source)
XLA Modules:
  0.0 504.3 jit_solution(13130272957411893450)
XLA Ops:
  44.3 9.0 %fusion.169 = f32[1,64,16,128]{1,0,3,2:T(1,128)S(1)} fusion(bf16[1,64,18,130]{1,0,3,2:T(2,128)(2,1)} %copy.294, bf16[64,64,3,3]{1,0,3,2:T(8,128)(2,1)S(1)} %copy-done), kind=kOutput, calls=%fused_computation.264 | convolution fusion | flops 150994944 | bytes 897536 | tf_op jit(solution)/shard_map/conv_general_dilated | solution.py:163
  74.4 10.0 %collective-permute-start.22 = (bf16[64,10,1]{0,2,1:T(2,128)(2,1)S(1)}, bf16[64,10,1]{0,2,1:T(2,128)(2,1)S(1)}, u32[]{:S(2)}, u32[]{:S(2)}) collective-permute-start(bf16[64,10,1]{0,2,1:T(2,128)(2,1)S(1)} %get-tuple-element.76), channel_id=1, source_target_pairs={{0,1},{1,2},{2,3},{3,4},{4,5},{5,6},{6,7},{7,8},{8,9},{9,10},{10,1... | collective-permute-start | bytes 3848 | tf_op jit(solution)/shard_map/ppermute | solution.py:156
  86.3 40.9 %collective-permute-done.23 = bf16[64,10,1]{0,2,1:T(2,128)(2,1)S(1)} collective-permute-done((bf16[64,10,1]{0,2,1:T(2,128)(2,1)S(1)}, bf16[64,10,1]{0,2,1:T(2,128)(2,1)S(1)}, u32[]{:S(2)}, u32[]{:S(2)}) %collective-permute-start.23) | collective-permute-done | bytes 1312 | tf_op jit(solution)/shard_map/ppermute | solution.py:157
  145.2 13.6 %copy.339 = f32[128,64,3,3]{3,2,1,0:T(4,128)} copy(f32[128,64,3,3]{0,1,3,2:T(8,128)S(1)} %pad_maximum_fusion.4) | data formatting | bytes 589824 | tf_op jit(solution)/shard_map/stack | solution.py:191
  158.8 14.0 %reshape.78 = f32[576,128]{1,0:T(8,128)} reshape(f32[128,64,3,3]{3,2,1,0:T(4,128)} %copy.339) | data formatting | bytes 589824 | tf_op jit(solution)/shard_map/reshape | solution.py:260
  177.8 8.3 %collective-permute-start.26 = (bf16[128,10,1]{0,2,1:T(2,128)(2,1)S(1)}, bf16[128,10,1]{0,2,1:T(2,128)(2,1)S(1)}, u32[]{:S(2)}, u32[]{:S(2)}) collective-permute-start(bf16[128,10,1]{0,2,1:T(2,128)(2,1)S(1)} %get-tuple-element.74), channel_id=1, source_target_pairs={{0,1},{1,2},{2,3},{3,4},{4,5},{5,6},{6,7},{7,8},{8,9},{9,10},{10,1... | collective-permute-start | bytes 7688 | tf_op jit(solution)/shard_map/ppermute | solution.py:156
  223.6 6.0 %copy.338 = f32[64,64,3,3]{3,2,1,0:T(4,128)} copy(f32[64,64,3,3]{1,0,3,2:T(8,128)S(1)} %pad_maximum_fusion.3) | data formatting | bytes 294912 | tf_op jit(solution)/shard_map/stack | solution.py:191
  229.7 7.5 %reshape.77 = f32[288,128]{1,0:T(8,128)S(1)} reshape(f32[64,64,3,3]{3,2,1,0:T(4,128)} %copy.338) | data formatting | bytes 294912 | tf_op jit(solution)/shard_map/reshape | solution.py:260
  237.3 8.8 %copy.349 = f32[64,128,3,3]{3,2,1,0:T(4,128)} copy(f32[64,128,3,3]{1,0,3,2:T(8,128)S(1)} %pad_maximum_fusion.5) | data formatting | bytes 589824 | tf_op jit(solution)/shard_map/stack | solution.py:191
  246.1 13.4 %reshape.79 = f32[576,128]{1,0:T(8,128)S(1)} reshape(f32[64,128,3,3]{3,2,1,0:T(4,128)} %copy.349) | data formatting | bytes 589824 | tf_op jit(solution)/shard_map/reshape | solution.py:260
  261.2 7.8 %collective-permute-start.30 = (bf16[64,18,1]{2,1,0:T(8,128)(2,1)}, bf16[64,18,1]{2,1,0:T(8,128)(2,1)}, u32[]{:S(2)}, u32[]{:S(2)}) collective-permute-start(bf16[64,18,1]{2,1,0:T(8,128)(2,1)} %get-tuple-element.48), channel_id=1, source_target_pairs={{0,1},{1,2},{2,3},{3,4},{4,5},{5,6},{6,7},{7,8},{8,9},{9,10},{10,1... | collective-permute-start | bytes 6920 | tf_op jit(solution)/shard_map/ppermute | solution.py:156
  276.7 7.8 %collective-permute-done.14 = bf16[64,18,1]{2,1,0:T(8,128)(2,1)S(1)} collective-permute-done((bf16[64,18,1]{2,1,0:T(8,128)(2,1)S(1)}, bf16[64,18,1]{2,1,0:T(8,128)(2,1)S(1)}, u32[]{:S(2)}, u32[]{:S(2)}) %collective-permute-start.14) | collective-permute-done | bytes 2336 | tf_op jit(solution)/shard_map/ppermute | solution.py:156
  284.4 8.1 %collective-permute-done.15 = bf16[64,18,1]{2,1,0:T(8,128)(2,1)S(1)} collective-permute-done((bf16[64,18,1]{2,1,0:T(8,128)(2,1)S(1)}, bf16[64,18,1]{2,1,0:T(8,128)(2,1)S(1)}, u32[]{:S(2)}, u32[]{:S(2)}) %collective-permute-start.15) | collective-permute-done | bytes 2336 | tf_op jit(solution)/shard_map/ppermute | solution.py:157
  295.7 8.2 %copy.368 = f32[64,64,3,3]{3,2,1,0:T(4,128)} copy(f32[64,64,3,3]{0,1,3,2:T(8,128)S(1)} %pad_maximum_fusion.6) | data formatting | bytes 294912 | tf_op jit(solution)/shard_map/stack | solution.py:191
  303.9 7.4 %reshape.80 = f32[288,128]{1,0:T(8,128)S(1)} reshape(f32[64,64,3,3]{3,2,1,0:T(4,128)} %copy.368) | data formatting | bytes 294912 | tf_op jit(solution)/shard_map/reshape | solution.py:260
  311.4 109.4 %shard_map.109 = f32[128,16,128]{2,1,0:T(8,128)S(1)} custom-call(f32[128,16,128]{2,1,0:T(8,128)S(1)} %bitcast.209), custom_call_target="tpu_custom_call" | custom-call | flops 1000000 | bytes 4000000 | tf_op jit(solution)/shard_map/pallas_call | solution.py:126
  433.2 6.0 %mul.214 = f32[64,64,3,3]{3,2,1,0:T(4,128)} reshape(f32[18,16,128]{2,1,0:T(8,128)S(1)} %copy-done.10) | data formatting | bytes 294912 | tf_op jit(solution)/shard_map/mul | solution.py:278
  439.2 7.6 %copy.374 = f32[64,64,3,3]{1,0,3,2:T(8,128)} copy(f32[64,64,3,3]{3,2,1,0:T(4,128)} %mul.214) | data formatting | bytes 294912
  446.8 6.2 %mul.207 = f32[64,64,3,3]{3,2,1,0:T(4,128)} reshape(f32[18,16,128]{2,1,0:T(8,128)S(1)} %get-tuple-element.37) | data formatting | bytes 294912 | tf_op jit(solution)/shard_map/mul | solution.py:275
  453.0 7.6 %copy.371 = f32[64,64,3,3]{1,0,3,2:T(8,128)} copy(f32[64,64,3,3]{3,2,1,0:T(4,128)} %mul.207) | data formatting | bytes 294912
  460.6 10.9 %mul.212 = f32[64,128,3,3]{3,2,1,0:T(4,128)} reshape(f32[36,16,128]{2,1,0:T(8,128)S(1)} %copy-done.7) | data formatting | bytes 589824 | tf_op jit(solution)/shard_map/mul | solution.py:277
  471.5 10.1 %copy.373 = f32[64,128,3,3]{1,0,3,2:T(8,128)} copy(f32[64,128,3,3]{3,2,1,0:T(4,128)} %mul.212) | data formatting | bytes 589824
  481.5 10.9 %mul.210 = f32[128,64,3,3]{3,2,1,0:T(4,128)} reshape(f32[36,16,128]{2,1,0:T(8,128)S(1)} %copy-done.6) | data formatting | bytes 589824 | tf_op jit(solution)/shard_map/mul | solution.py:276
  492.4 11.7 %copy.372 = f32[128,64,3,3]{0,1,3,2:T(8,128)} copy(f32[128,64,3,3]{3,2,1,0:T(4,128)} %mul.210) | data formatting | bytes 589824
  (264 shorter events, 151.0 us)
Async XLA Ops:
  1.7 16.7 %collective-permute-start.16 = (bf16[64,1,128]{2,0,1:T(8,128)(2,1)S(1)}, bf16[64,1,128]{2,0,1:T(8,128)(2,1)S(1)}, u32[]{:S(2)}, u32[]{:S(2)}) collective-permute-start(bf16[64,1,128]{2,0,1:T(8,128)(2,1)S(1)} %copy.457), channel_id=1, source_target_pairs={{0,16},{16,32},{32,48},{48,64},{64,80},{80,96},{96,112},{112,128},... | collective-permute-start | bytes 49160 | tf_op jit(solution)/shard_map/ppermute | solution.py:156
  6.7 12.9 %collective-permute-start.17 = (bf16[64,1,128]{2,0,1:T(8,128)(2,1)S(1)}, bf16[64,1,128]{2,0,1:T(8,128)(2,1)S(1)}, u32[]{:S(2)}, u32[]{:S(2)}) collective-permute-start(bf16[64,1,128]{2,0,1:T(8,128)(2,1)S(1)} %copy.458), channel_id=1, source_target_pairs={{16,0},{32,16},{48,32},{64,48},{80,64},{96,80},{112,96},{128,112},... | collective-permute-start | bytes 49160 | tf_op jit(solution)/shard_map/ppermute | solution.py:157
  23.5 16.7 %collective-permute-start.2 = (bf16[64,18,1]{2,0,1:T(8,128)(2,1)}, bf16[64,18,1]{2,0,1:T(8,128)(2,1)S(1)}, u32[]{:S(2)}, u32[]{:S(2)}) collective-permute-start(bf16[64,18,1]{2,0,1:T(8,128)(2,1)} %get-tuple-element.56), channel_id=1, source_target_pairs={{0,1},{1,2},{2,3},{3,4},{4,5},{5,6},{6,7},{7,8},{8,9},{9,10},{10,1... | collective-permute-start | bytes 6920 | tf_op jit(solution)/shard_map/ppermute | solution.py:156
  27.5 12.7 %collective-permute-start.3 = (bf16[64,18,1]{2,0,1:T(8,128)(2,1)}, bf16[64,18,1]{2,0,1:T(8,128)(2,1)}, u32[]{:S(2)}, u32[]{:S(2)}) collective-permute-start(bf16[64,18,1]{2,0,1:T(8,128)(2,1)} %get-tuple-element.57), channel_id=1, source_target_pairs={{1,0},{2,1},{3,2},{4,3},{5,4},{6,5},{7,6},{8,7},{9,8},{10,9},{11,1... | collective-permute-start | bytes 6920 | tf_op jit(solution)/shard_map/ppermute | solution.py:157
  54.5 12.9 %collective-permute-start.4 = (bf16[64,1,64]{2,0,1:T(8,128)(2,1)S(1)}, bf16[64,1,64]{2,0,1:T(8,128)(2,1)S(1)}, u32[]{:S(2)}, u32[]{:S(2)}) collective-permute-start(bf16[64,1,64]{2,0,1:T(8,128)(2,1)S(1)} %get-tuple-element.88), channel_id=1, source_target_pairs={{0,16},{16,32},{32,48},{48,64},{64,80},{80,96},{96,112},{112,128},... | collective-permute-start | bytes 24584 | tf_op jit(solution)/shard_map/ppermute | solution.py:156
  61.7 12.7 %collective-permute-start.20 = (bf16[64,1,64]{0,2,1:T(8,128)(2,1)S(1)}, bf16[64,1,64]{0,2,1:T(8,128)(2,1)S(1)}, u32[]{:S(2)}, u32[]{:S(2)}) collective-permute-start(bf16[64,1,64]{0,2,1:T(8,128)(2,1)S(1)} %get-tuple-element.84), channel_id=1, source_target_pairs={{0,16},{16,32},{32,48},{48,64},{64,80},{80,96},{96,112},{112,128},... | collective-permute-start | bytes 24584 | tf_op jit(solution)/shard_map/ppermute | solution.py:156
  67.6 18.3 %collective-permute-start.6 = (bf16[64,10,1]{2,0,1:T(8,128)(2,1)S(1)}, bf16[64,10,1]{2,0,1:T(8,128)(2,1)S(1)}, u32[]{:S(2)}, u32[]{:S(2)}) collective-permute-start(bf16[64,10,1]{2,0,1:T(8,128)(2,1)S(1)} %get-tuple-element.80), channel_id=1, source_target_pairs={{0,1},{1,2},{2,3},{3,4},{4,5},{5,6},{6,7},{7,8},{8,9},{9,10},{10,1... | collective-permute-start | bytes 3848 | tf_op jit(solution)/shard_map/ppermute | solution.py:156
  73.0 12.9 %collective-permute-start.7 = (bf16[64,10,1]{2,0,1:T(8,128)(2,1)S(1)}, bf16[64,10,1]{2,0,1:T(8,128)(2,1)S(1)}, u32[]{:S(2)}, u32[]{:S(2)}) collective-permute-start(bf16[64,10,1]{2,0,1:T(8,128)(2,1)S(1)} %get-tuple-element.81), channel_id=1, source_target_pairs={{1,0},{2,1},{3,2},{4,3},{5,4},{6,5},{7,6},{8,7},{9,8},{10,9},{11,1... | collective-permute-start | bytes 3848 | tf_op jit(solution)/shard_map/ppermute | solution.py:157
  84.4 42.9 %collective-permute-start.23 = (bf16[64,10,1]{0,2,1:T(2,128)(2,1)S(1)}, bf16[64,10,1]{0,2,1:T(2,128)(2,1)S(1)}, u32[]{:S(2)}, u32[]{:S(2)}) collective-permute-start(bf16[64,10,1]{0,2,1:T(2,128)(2,1)S(1)} %get-tuple-element.77), channel_id=1, source_target_pairs={{1,0},{2,1},{3,2},{4,3},{5,4},{6,5},{7,6},{8,7},{9,8},{10,9},{11,1... | collective-permute-start | bytes 3848 | tf_op jit(solution)/shard_map/ppermute | solution.py:157
  132.1 40.6 %collective-permute-start.8 = (bf16[128,1,64]{0,2,1:T(8,128)(2,1)S(1)}, bf16[128,1,64]{0,2,1:T(8,128)(2,1)S(1)}, u32[]{:S(2)}, u32[]{:S(2)}) collective-permute-start(bf16[128,1,64]{0,2,1:T(8,128)(2,1)S(1)} %get-tuple-element.86), channel_id=1, source_target_pairs={{0,16},{16,32},{32,48},{48,64},{64,80},{80,96},{96,112},{112,128},... | collective-permute-start | bytes 49160 | tf_op jit(solution)/shard_map/ppermute | solution.py:156
  137.2 35.6 %collective-permute-start.9 = (bf16[128,1,64]{0,2,1:T(8,128)(2,1)S(1)}, bf16[128,1,64]{0,2,1:T(8,128)(2,1)S(1)}, u32[]{:S(2)}, u32[]{:S(2)}) collective-permute-start(bf16[128,1,64]{0,2,1:T(8,128)(2,1)S(1)} %get-tuple-element.87), channel_id=1, source_target_pairs={{16,0},{32,16},{48,32},{64,48},{80,64},{96,80},{112,96},{128,112},... | collective-permute-start | bytes 49160 | tf_op jit(solution)/shard_map/ppermute | solution.py:157
  139.1 38.6 %collective-permute-start.24 = (bf16[128,1,64]{0,2,1:T(8,128)(2,1)S(1)}, bf16[128,1,64]{0,2,1:T(8,128)(2,1)S(1)}, u32[]{:S(2)}, u32[]{:S(2)}) collective-permute-start(bf16[128,1,64]{0,2,1:T(8,128)(2,1)S(1)} %get-tuple-element.82), channel_id=1, source_target_pairs={{0,16},{16,32},{32,48},{48,64},{64,80},{80,96},{96,112},{112,128},... | collective-permute-start | bytes 49160 | tf_op jit(solution)/shard_map/ppermute | solution.py:156
  142.8 35.0 %collective-permute-start.25 = (bf16[128,1,64]{0,2,1:T(8,128)(2,1)S(1)}, bf16[128,1,64]{0,2,1:T(8,128)(2,1)S(1)}, u32[]{:S(2)}, u32[]{:S(2)}) collective-permute-start(bf16[128,1,64]{0,2,1:T(8,128)(2,1)S(1)} %get-tuple-element.83), channel_id=1, source_target_pairs={{16,0},{32,16},{48,32},{64,48},{80,64},{96,80},{112,96},{128,112},... | collective-permute-start | bytes 49160 | tf_op jit(solution)/shard_map/ppermute | solution.py:157
  172.8 16.6 %collective-permute-start.10 = (bf16[128,10,1]{0,2,1:T(2,128)(2,1)S(1)}, bf16[128,10,1]{0,2,1:T(2,128)(2,1)S(1)}, u32[]{:S(2)}, u32[]{:S(2)}) collective-permute-start(bf16[128,10,1]{0,2,1:T(2,128)(2,1)S(1)} %get-tuple-element.78), channel_id=1, source_target_pairs={{0,1},{1,2},{2,3},{3,4},{4,5},{5,6},{6,7},{7,8},{8,9},{9,10},{10,1... | collective-permute-start | bytes 7688 | tf_op jit(solution)/shard_map/ppermute | solution.py:156
  176.4 13.0 %collective-permute-start.11 = (bf16[128,10,1]{0,2,1:T(2,128)(2,1)S(1)}, bf16[128,10,1]{0,2,1:T(2,128)(2,1)S(1)}, u32[]{:S(2)}, u32[]{:S(2)}) collective-permute-start(bf16[128,10,1]{0,2,1:T(2,128)(2,1)S(1)} %get-tuple-element.79), channel_id=1, source_target_pairs={{1,0},{2,1},{3,2},{4,3},{5,4},{6,5},{7,6},{8,7},{9,8},{10,9},{11,1... | collective-permute-start | bytes 7688 | tf_op jit(solution)/shard_map/ppermute | solution.py:157
  177.8 16.6 %collective-permute-start.26 = (bf16[128,10,1]{0,2,1:T(2,128)(2,1)S(1)}, bf16[128,10,1]{0,2,1:T(2,128)(2,1)S(1)}, u32[]{:S(2)}, u32[]{:S(2)}) collective-permute-start(bf16[128,10,1]{0,2,1:T(2,128)(2,1)S(1)} %get-tuple-element.74), channel_id=1, source_target_pairs={{0,1},{1,2},{2,3},{3,4},{4,5},{5,6},{6,7},{7,8},{8,9},{9,10},{10,1... | collective-permute-start | bytes 7688 | tf_op jit(solution)/shard_map/ppermute | solution.py:156
  205.7 53.9 %collective-permute-start.12 = (bf16[64,1,128]{2,1,0:T(2,128)(2,1)S(1)}, bf16[64,1,128]{2,1,0:T(2,128)(2,1)S(1)}, u32[]{:S(2)}, u32[]{:S(2)}) collective-permute-start(bf16[64,1,128]{2,1,0:T(2,128)(2,1)S(1)} %get-tuple-element.66), channel_id=1, source_target_pairs={{0,16},{16,32},{32,48},{48,64},{64,80},{80,96},{96,112},{112,128},... | collective-permute-start | bytes 49160 | tf_op jit(solution)/shard_map/ppermute | solution.py:156
  210.8 48.8 %collective-permute-start.13 = (bf16[64,1,128]{2,1,0:T(2,128)(2,1)S(1)}, bf16[64,1,128]{2,1,0:T(2,128)(2,1)S(1)}, u32[]{:S(2)}, u32[]{:S(2)}) collective-permute-start(bf16[64,1,128]{2,1,0:T(2,128)(2,1)S(1)} %get-tuple-element.67), channel_id=1, source_target_pairs={{16,0},{32,16},{48,32},{64,48},{80,64},{96,80},{112,96},{128,112},... | collective-permute-start | bytes 49160 | tf_op jit(solution)/shard_map/ppermute | solution.py:157
  212.7 47.4 %collective-permute-start.28 = (bf16[64,1,128]{2,1,0:T(2,128)(2,1)S(1)}, bf16[64,1,128]{2,1,0:T(2,128)(2,1)S(1)}, u32[]{:S(2)}, u32[]{:S(2)}) collective-permute-start(bf16[64,1,128]{2,1,0:T(2,128)(2,1)S(1)} %get-tuple-element.60), channel_id=1, source_target_pairs={{0,16},{16,32},{32,48},{48,64},{64,80},{80,96},{96,112},{112,128},... | collective-permute-start | bytes 49160 | tf_op jit(solution)/shard_map/ppermute | solution.py:156
  216.3 43.7 %collective-permute-start.29 = (bf16[64,1,128]{2,1,0:T(2,128)(2,1)S(1)}, bf16[64,1,128]{2,1,0:T(2,128)(2,1)S(1)}, u32[]{:S(2)}, u32[]{:S(2)}) collective-permute-start(bf16[64,1,128]{2,1,0:T(2,128)(2,1)S(1)} %get-tuple-element.61), channel_id=1, source_target_pairs={{16,0},{32,16},{48,32},{64,48},{80,64},{96,80},{112,96},{128,112},... | collective-permute-start | bytes 49160 | tf_op jit(solution)/shard_map/ppermute | solution.py:157
  261.2 161.1 %collective-permute-start.30 = (bf16[64,18,1]{2,1,0:T(8,128)(2,1)}, bf16[64,18,1]{2,1,0:T(8,128)(2,1)}, u32[]{:S(2)}, u32[]{:S(2)}) collective-permute-start(bf16[64,18,1]{2,1,0:T(8,128)(2,1)} %get-tuple-element.48), channel_id=1, source_target_pairs={{0,1},{1,2},{2,3},{3,4},{4,5},{5,6},{6,7},{7,8},{8,9},{9,10},{10,1... | collective-permute-start | bytes 6920 | tf_op jit(solution)/shard_map/ppermute | solution.py:156
  269.0 153.3 %collective-permute-start.31 = (bf16[64,18,1]{2,1,0:T(8,128)(2,1)S(1)}, bf16[64,18,1]{2,1,0:T(8,128)(2,1)}, u32[]{:S(2)}, u32[]{:S(2)}) collective-permute-start(bf16[64,18,1]{2,1,0:T(8,128)(2,1)S(1)} %get-tuple-element.49), channel_id=1, source_target_pairs={{1,0},{2,1},{3,2},{4,3},{5,4},{6,5},{7,6},{8,7},{9,8},{10,9},{11,1... | collective-permute-start | bytes 6920 | tf_op jit(solution)/shard_map/ppermute | solution.py:157
  270.5 14.0 %collective-permute-start.14 = (bf16[64,18,1]{2,1,0:T(8,128)(2,1)S(1)}, bf16[64,18,1]{2,1,0:T(8,128)(2,1)S(1)}, u32[]{:S(2)}, u32[]{:S(2)}) collective-permute-start(bf16[64,18,1]{2,1,0:T(8,128)(2,1)S(1)} %get-tuple-element.50), channel_id=1, source_target_pairs={{0,1},{1,2},{2,3},{3,4},{4,5},{5,6},{6,7},{7,8},{8,9},{9,10},{10,1... | collective-permute-start | bytes 6920 | tf_op jit(solution)/shard_map/ppermute | solution.py:156
  274.6 17.9 %collective-permute-start.15 = (bf16[64,18,1]{2,1,0:T(8,128)(2,1)S(1)}, bf16[64,18,1]{2,1,0:T(8,128)(2,1)S(1)}, u32[]{:S(2)}, u32[]{:S(2)}) collective-permute-start(bf16[64,18,1]{2,1,0:T(8,128)(2,1)S(1)} %get-tuple-element.51), channel_id=1, source_target_pairs={{1,0},{2,1},{3,2},{4,3},{5,4},{6,5},{7,6},{8,7},{9,8},{10,9},{11,1... | collective-permute-start | bytes 6920 | tf_op jit(solution)/shard_map/ppermute | solution.py:157
  (41 other events, 469.1 us)

commit v2 on v1

--- a/solution.py
+++ b/solution.py
@@ -7,8 +7,384 @@
 from jax.experimental.pallas import tpu as pltpu
 from jax.sharding import PartitionSpec as P
 
-
 MESH = pl.DeviceIdType.MESH
+BF, F32 = jnp.bfloat16, jnp.float32
+VMEM = pl.BlockSpec(memory_space=pltpu.VMEM)
+GELU_SCALE = 0.7978845608028654
+GELU_CUBE = 0.044715
+REACH = 7
+
+
+def _pack_kernel(x_ref, cot_ref, rows_ref, left_ref, right_ref, flat):
+    lane = lax.broadcasted_iota(jnp.int32, (64, 128), 1) // 8
+    for field, ref in ((0, x_ref), (1, cot_ref)):
+        flat[...] = ref[...].astype(F32).reshape(1024, 128)
+        at = pl.ds(field * 64, 64)
+        left = jnp.zeros((64, 128), F32)
+        right = jnp.zeros((64, 128), F32)
+        for h in range(16):
+            row = flat[pl.ds(h, 64, stride=16), :]
+            rows_ref[h, at, :] = row.astype(BF)
+            left = jnp.where(lane == h, row if h == 0 else pltpu.roll(row, 8 * h, axis=1), left)
+            right = jnp.where(lane == h, row if h == 15 else pltpu.roll(row, 8 * h + 8, axis=1), right)
+        left_ref[at, :] = left.astype(BF)
+        right_ref[at, :] = right.astype(BF)
+
+
+def pack(level_input, cotangent):
+    return pl.pallas_call(
+        _pack_kernel,
+        out_shape=(
+            jax.ShapeDtypeStruct((16, 128, 128), BF),
+            jax.ShapeDtypeStruct((128, 128), BF),
+            jax.ShapeDtypeStruct((128, 128), BF),
+        ),
+        in_specs=[VMEM] * 2,
+        out_specs=(VMEM,) * 3,
+        scratch_shapes=[pltpu.VMEM((1024, 128), F32)],
+        compiler_params=pltpu.CompilerParams(vmem_limit_bytes=16 * 1024 * 1024),
+        cost_estimate=pl.CostEstimate(flops=1000000, bytes_accessed=1500000, transcendentals=0),
+    )(level_input, cotangent)
+
+
+def _rim_kernel(rows_ref, left_ref, right_ref, above_ref, below_ref, from_left_ref, from_right_ref,
+                send_sem, recv_sem):
+    row, col = lax.axis_index("rows"), lax.axis_index("cols")
+    height, width = lax.axis_size("rows"), lax.axis_size("cols")
+
+    def peer(dr, dc):
+        return ((row + dr + height) % height, (col + dc + width) % width)
+
+    around = [(dr, dc) for dr in (-1, 0, 1) for dc in (-1, 0, 1) if (dr, dc) != (0, 0)]
+    barrier = pltpu.get_barrier_semaphore()
+    for dr, dc in around:
+        pl.semaphore_signal(barrier, inc=1, device_id=peer(dr, dc), device_id_type=MESH)
+    pl.semaphore_wait(barrier, len(around))
+    plan = [
+        (rows_ref.at[pl.ds(0, REACH)], below_ref, (-1, 0)),
+        (rows_ref.at[pl.ds(16 - REACH, REACH)], above_ref, (1, 0)),
+    ]
+    for dr in (0, -1, 1):
+        plan.append((left_ref, from_right_ref.at[1 - dr], (dr, -1)))
+        plan.append((right_ref, from_left_ref.at[1 - dr], (dr, 1)))
+    copies = []
+    for k, (src, dst, offset) in enumerate(plan):
+        copies.append(pltpu.make_async_remote_copy(
+            src_ref=src, dst_ref=dst, send_sem=send_sem.at[k], recv_sem=recv_sem.at[k],
+            device_id=peer(*offset), device_id_type=MESH))
+        copies[-1].start()
+    for copy in copies:
+        copy.wait()
+
+
+def exchange(rows, left, right):
+    shape = lambda n: jax.ShapeDtypeStruct((n, 128, 128), BF)
+    return pl.pallas_call(
+        _rim_kernel,
+        out_shape=(shape(REACH), shape(REACH), shape(3), shape(3)),
+        in_specs=[VMEM] * 3,
+        out_specs=(VMEM,) * 4,
+        scratch_shapes=[pltpu.SemaphoreType.DMA((8,)), pltpu.SemaphoreType.DMA((8,))],
+        compiler_params=pltpu.CompilerParams(
+            collective_id=0, has_side_effects=True, vmem_limit_bytes=16 * 1024 * 1024),
+        cost_estimate=pl.CostEstimate(flops=1000, bytes_accessed=2000000, transcendentals=0),
+    )(rows, left, right)
+
+
+def _gelu_parts(x):
+    square = x * x
+    bend = jnp.tanh(GELU_SCALE * (x + GELU_CUBE * (x * square)))
+    half = 0.5 + 0.5 * bend
+    slope = half + (0.5 * GELU_SCALE) * x * (1.0 - bend * bend) * (1.0 + (3.0 * GELU_CUBE) * square)
+    return x * half, slope
+
+
+def _taps(x):
+    lanes = x.shape[1]
+    return jnp.concatenate(
+        [pltpu.roll(x, 1, axis=1).astype(BF), x.astype(BF), pltpu.roll(x, lanes - 1, axis=1).astype(BF)],
+        axis=0)
+
+
+def _dot(a, b):
+    return jnp.dot(a, b, preferred_element_type=F32)
+
+
+def _dot_t(a, b):
+    return lax.dot_general(a, b, (((1,), (1,)), ((), ())), preferred_element_type=F32)
+
+
+def _loop(first, last, step, unroll=1):
+    def body(i, carry):
+        step(i)
+        return carry
+    lax.fori_loop(first, last, body, 0, unroll=unroll)
+
+
+def _levels_kernel(edge_ref, rows_ref, above_ref, below_ref, from_left_ref, from_right_ref,
+                   ka_ref, kb_ref, kc_ref, kd_ref, result_ref, input_grad_ref, sums_ref,
+                   wa, wat, wb, wbt, wc, wct, wd, wdt, pool, spread,
+                   x3, cot3, parts, cparts, hidden, slope_a, slope_b, coarse3, middle3, coarse_out,
+                   joined3, grad_joined, grad_coarse3, grad_b3, grad_pool, up, grad_a3,
+                   pad_a, pad_b, pad_c, pad_d, flat, acc):
+    top, bottom = edge_ref[0], edge_ref[1]
+    low, high = edge_ref[2], edge_ref[3]
+    f_lane = lax.broadcasted_iota(jnp.int32, (1, 256), 1)
+    c_lane = lax.broadcasted_iota(jnp.int32, (1, 128), 1)
+    f_mask = ((f_lane < 136 - 8 * high) | (f_lane >= 248 + 8 * low)).astype(F32)
+    c_mask = ((c_lane < 68 - 4 * high) | (c_lane >= 124 + 4 * low)).astype(F32)
+    own_c = (c_lane < 64).astype(F32)
+
+    for a in range(3):
+        for b in range(3):
+            tap, flip = 3 * a + b, 8 - (3 * a + b)
+            at64, at128 = pl.ds(64 * a, 64), pl.ds(128 * a, 128)
+            col64, col128 = slice(64 * b, 64 * b + 64), slice(128 * b, 128 * b + 128)
+            wa[at64, col64] = ka_ref[tap]
+            wd[at64, col64] = kd_ref[tap]
+            wc[at64, col128] = kc_ref[tap]
+            wbt[at64, col128] = kb_ref[flip]
+            wat[at64, col64] = ka_ref[flip].astype(F32).T.astype(BF)
+            wdt[at64, col64] = kd_ref[flip].astype(F32).T.astype(BF)
+            wb[at128, col64] = kb_ref[tap].astype(F32).T.astype(BF)
+            wct[at128, col64] = kc_ref[flip].astype(F32).T.astype(BF)
+    cell = lax.broadcasted_iota(jnp.int32, (512, 128), 0)
+    block = lax.broadcasted_iota(jnp.int32, (512, 128), 1)
+    pool[...] = ((cell % 256) // 2 == block).astype(F32).astype(BF)
+    cell = lax.broadcasted_iota(jnp.int32, (128, 256), 1)
+    block = lax.broadcasted_iota(jnp.int32, (128, 256), 0)
+    spread[...] = (cell // 2 == block).astype(F32).astype(BF)
+
+    side_lane = lax.broadcasted_iota(jnp.int32, (128, 128), 1)
+    for i in range(30):
+        h = i - REACH
+        if h < 0:
+            center, j, p = above_ref[h + REACH], 0, h + 16
+        elif h < 16:
+            center, j, p = rows_ref[h], 1, h
+        else:
+            center, j, p = below_ref[h - 16], 2, h - 16
+        right = from_right_ref[j].astype(F32)
+        left = from_left_ref[j].astype(F32)
+        right = right if p == 0 else pltpu.roll(right, 128 - 8 * p, axis=1)
+        left = left if p == 15 else pltpu.roll(left, 120 - 8 * p, axis=1)
+        side = jnp.where(side_lane < 8, right, left)
+        wide = jnp.concatenate([center.astype(F32), side], axis=1) * f_mask
+        x3[i] = _taps(wide[:64])
+        cot3[i] = _taps(wide[64:])
+
+    def clear(ref, top_rows, total):
+        @pl.when(top == 1)
+        def _():
+            ref[pl.ds(0, top_rows)] = jnp.zeros((top_rows,) + ref.shape[1:], ref.dtype)
+
+        @pl.when(bottom == 1)
+        def _():
+            ref[pl.ds(total - top_rows, top_rows)] = jnp.zeros((top_rows,) + ref.shape[1:], ref.dtype)
+
+    clear(x3, 7, 30)
+    clear(cot3, 7, 30)
+
+    def conv(weights, source, into, rows, unroll):
+        def step(i):
+            into[i] = _dot(weights[...], source[i])
+        _loop(0, rows, step, unroll)
+
+    def gathered(from_, i, outs):
+        return from_[i - 1, 0:outs] + from_[i, outs:2 * outs] + from_[i + 1, 2 * outs:3 * outs]
+
+    conv(wa, x3, parts, 30, 5)
+
+    def first(with_slope):
+        def step(k):
+            for s in range(2):
+                pre = gathered(parts, 2 * k + 1 + s, 64)
+                value, slope = _gelu_parts(pre)
+                hidden[k, :, 256 * s:256 * s + 256] = (value * f_mask).astype(BF)
+                if with_slope:
+                    slope_a[k - 2, :, 256 * s:256 * s + 256] = slope
+        return step
+    _loop(0, 2, first(False))
+    _loop(2, 12, first(True))
+    _loop(12, 14, first(False))
+    clear(hidden, 3, 14)
+
+    def pool_step(k):
+        coarse3[k] = _taps((_dot(hidden[k], pool[...]) * 0.25).astype(BF).astype(F32))
+    _loop(0, 14, pool_step, 7)
+
+    conv(wb, coarse3, cparts, 14, 7)
+
+    def second(k):
+        value, slope = _gelu_parts(gathered(cparts, k + 1, 128))
+        middle3[k] = _taps(value * c_mask)
+        slope_b[k] = slope
+    _loop(0, 12, second, 2)
+    clear(middle3, 2, 12)
+
+    def third(k):
+        cparts[k, 0:192] = _dot(wc[...], middle3[k])
+    _loop(0, 12, third, 6)
+
+    def third_sum(k):
+        coarse_out[k] = (gathered(cparts, k + 1, 64) * c_mask).astype(BF)
+    _loop(0, 10, third_sum, 5)
+    clear(coarse_out, 1, 10)
+
+    def spread_step(source):
+        def step(k):
+            up[k] = _dot(source[k], spread[...])
+        return step
+    _loop(0, 10, spread_step(coarse_out), 5)
+
+    def join(k, s):
+        both = hidden[k + 2, :, 256 * s:256 * s + 256].astype(F32) + up[k]
+        joined3[2 * k - 1 + s] = _taps(both)[:, 0:128]
+    join(0, 1)
+
+    def join_step(k):
+        join(k, 0)
+        join(k, 1)
+    _loop(1, 9, join_step, 2)
+    join(9, 0)
+
+    def out_rows(weights, source, ref):
+        def step(i):
+            parts[i, :, 0:128] = _dot(weights[...], source[i])
+        _loop(0, 18, step, 6)
+        for h in range(16):
+            flat[pl.ds(h, 64, stride=16), :] = gathered(
+                parts.at[:, :, pl.ds(0, 128)], h + 1, 64)
+        ref[...] = flat[...].reshape(64, 16, 128).astype(BF)
+
+    out_rows(wd, joined3, result_ref)
+
+    conv(wdt, cot3, parts, 30, 5)
+
+    def back_first(k):
+        for s in range(2):
+            grad = gathered(parts, 2 * k + 1 + s, 64) * f_mask
+            grad_joined[k, :, 256 * s:256 * s + 256] = grad.astype(BF)
+    _loop(0, 14, back_first, 2)
+    clear(grad_joined, 3, 14)
+
+    def back_pool(k):
+        grad_coarse3[k] = _taps(_dot(grad_joined[k], pool[...]).astype(BF).astype(F32))
+    _loop(0, 14, back_pool, 7)
+    conv(wct, grad_coarse3, cparts, 14, 7)
+
+    def back_second(k):
+        grad_b3[k] = _taps(slope_b[k] * gathered(cparts, k + 1, 128) * c_mask)
+    _loop(0, 12, back_second, 2)
+    clear(grad_b3, 2, 12)
+
+    def back_third(k):
+        cparts[k, 0:192] = _dot(wbt[...], grad_b3[k])
+    _loop(0, 12, back_third, 6)
+
+    def back_third_sum(k):
+        grad_pool[k] = gathered(cparts, k + 1, 64).astype(BF)
+    _loop(0, 10, back_third_sum, 5)
+    _loop(0, 10, spread_step(grad_pool), 5)
+
+    def back_join(k, s):
+        at = slice(256 * s, 256 * s + 256)
+        grad = grad_joined[k + 2, :, at].astype(F32) + 0.25 * up[k]
+        grad_a3[2 * k - 1 + s] = _taps(slope_a[k, :, at] * grad * f_mask)[:, 0:128]
+    back_join(0, 1)
+
+    def back_join_step(k):
+        back_join(k, 0)
+        back_join(k, 1)
+    _loop(1, 9, back_join_step, 2)
+    back_join(9, 0)
+    clear(grad_a3, 1, 18)
+    out_rows(wat, grad_a3, input_grad_ref)
+
+    for pad, before in ((pad_a, 2), (pad_d, 2), (pad_c, 2)):
+        pad[pl.ds(0, before)] = jnp.zeros((before,) + pad.shape[1:], BF)
+        size = pad.shape[0]
+        pad[pl.ds(size - before, before)] = jnp.zeros((before,) + pad.shape[1:], BF)
+    _loop(0, 16, lambda h: pad_a.__setitem__(h + 2, grad_a3[h + 1, 64:128, :]), 4)
+    _loop(0, 16, lambda h: pad_d.__setitem__(h + 2, cot3[h + 7, 64:128, 0:128]), 4)
+    _loop(0, 8, lambda k: pad_b.__setitem__(
+        k, (grad_b3[k + 2, 128:256, :].astype(F32) * own_c).astype(BF)), 4)
+    _loop(0, 8, lambda k: pad_c.__setitem__(
+        k + 2, (grad_coarse3[k + 3, 64:128, :].astype(F32) * own_c).astype(BF)), 4)
+
+    def stacked(pad, j):
+        return jnp.concatenate([pad[j + 2], pad[j + 1], pad[j]], axis=0)
+
+    def pair(one, j):
+        return jnp.concatenate([one(2 * j), one(2 * j + 1)], axis=1)
+
+    def weight_grad(pad, window, pairs, into):
+        def step(j):
+            into[...] += _dot_t(pair(lambda i: stacked(pad, i), j), pair(window, j))
+        into[...] = jnp.zeros(into.shape, F32)
+        _loop(0, pairs, step, pairs)
+
+    sums_ref[pl.ds(1728, 320), :] = jnp.zeros((320, 128), F32)
+    acc_a, acc_d = acc.at[0:192, 0:192], acc.at[0:192, 256:448]
+    acc_a = acc.at[pl.ds(0, 192), pl.ds(0, 256)]
+    acc_d = acc.at[pl.ds(0, 192), pl.ds(256, 256)]
+    for pad, window, at in ((pad_a, lambda i: x3[i + 6, :, 0:128], 0),
+                            (pad_d, lambda i: joined3[i], 256)):
+        def step(j, pad=pad, window=window, at=at):
+            acc[0:192, at:at + 192] += _dot_t(pair(lambda i: stacked(pad, i), j), pair(window, j))
+        acc[0:192, at:at + 192] = jnp.zeros((192, 192), F32)
+        _loop(0, 9, step, 3)
+    for a in range(3):
+        for b in range(3):
+            rows = slice(64 * a, 64 * a + 64)
+            sums_ref[pl.ds(64 * (3 * a + b), 64), :] = jnp.concatenate(
+                [acc[rows, 64 * b:64 * b + 64], acc[rows, 256 + 64 * b:320 + 64 * b]], axis=1)
+
+    sums_ref[pl.ds(576, 576), :] = jnp.zeros((576, 128), F32)
+
+    def b_step(j):
+        def window(k):
+            return jnp.concatenate([coarse3[k + 2], coarse3[k + 3], coarse3[k + 4]], axis=0)
+        sums_ref[pl.ds(576, 576), :] += _dot_t(pair(window, j), pair(lambda k: pad_b[k], j))
+    _loop(0, 4, b_step, 2)
+
+    acc[0:192, 0:384] = jnp.zeros((192, 384), F32)
+
+    def c_step(j):
+        acc[0:192, 0:384] += _dot_t(
+            pair(lambda i: stacked(pad_c, i), j), pair(lambda i: middle3[i + 1], j))
+    _loop(0, 5, c_step, 1)
+    for a in range(3):
+        for b in range(3):
+            sums_ref[pl.ds(1152 + 64 * (3 * a + b), 64), :] = acc[64 * a:64 * a + 64, 128 * b:128 * b + 128]
+
+
+def levels(edges, rows, above, below, from_left, from_right, ka, kb, kc, kd):
+    scratch = [
+        ((192, 192), BF), ((192, 192), BF), ((384, 192), BF), ((192, 384), BF),
+        ((192, 384), BF), ((384, 192), BF), ((192, 192), BF), ((192, 192), BF),
+        ((512, 128), BF), ((128, 256), BF),
+        ((30, 192, 256), BF), ((30, 192, 256), BF), ((30, 192, 256), F32), ((14, 384, 128), F32),
+        ((14, 64, 512), BF), ((10, 64, 512), F32), ((12, 128, 128), F32),
+        ((14, 192, 128), BF), ((12, 384, 128), BF), ((10, 64, 128), BF),
+        ((18, 192, 128), BF), ((14, 64, 512), BF), ((14, 192, 128), BF), ((12, 384, 128), BF),
+        ((10, 64, 128), BF), ((10, 64, 256), F32), ((18, 192, 128), BF),
+        ((20, 64, 128), BF), ((8, 128, 128), BF), ((12, 64, 128), BF), ((20, 64, 128), BF),
+        ((1024, 128), F32), ((192, 512), F32),
+    ]
+    return pl.pallas_call(
+        _levels_kernel,
+        out_shape=(
+            jax.ShapeDtypeStruct((64, 16, 128), BF),
+            jax.ShapeDtypeStruct((64, 16, 128), BF),
+            jax.ShapeDtypeStruct((2048, 128), F32),
+        ),
+        in_specs=[pl.BlockSpec(memory_space=pltpu.SMEM)] + [VMEM] * 9,
+        out_specs=(VMEM,) * 3,
+        scratch_shapes=[pltpu.VMEM(shape, dtype) for shape, dtype in scratch],
+        compiler_params=pltpu.CompilerParams(vmem_limit_bytes=48 * 1024 * 1024),
+        cost_estimate=pl.CostEstimate(flops=2000000000, bytes_accessed=8000000, transcendentals=1000000),
+    )(edges, rows, above, below, from_left, from_right, ka, kb, kc, kd)
 
 
 def _reduce_kernel(x_ref, out_ref, pair_out, pair_in, plane_out, plane_in, own, near_in, far, whole,
@@ -146,124 +522,25 @@
     )(tiles)
 
 
-def with_halo(array, sides, width):
-    for axis, dim in sides:
-        peers, length = (lax.axis_size(axis), array.shape[dim])
-        up = [(i, (i + 1) % peers) for i in range(peers - 1)]
-        down = [(j, i) for i, j in up]
-        last = lax.slice_in_dim(array, length - width, length, axis=dim)
-        initial = lax.slice_in_dim(array, 0, width, axis=dim)
-        before = lax.ppermute(last, axis, up)
-        after = lax.ppermute(initial, axis, down)
-        array = jnp.concatenate([before, array, after], axis=dim)
-    return array
-
-
-def conv_valid(padded, kernel):
-    result = lax.conv_general_dilated(
-        padded[None],
-        kernel,
-        (1, 1),
-        "VALID",
-        dimension_numbers=("NCHW", "OIHW", "NCHW"),
-        preferred_element_type=jnp.float32,
-    )
-    return result[0]
-
-
-def kernel_grad(padded, upstream):
-    height = upstream.shape[1]
-    width_cells = upstream.shape[2]
-    tap_list = []
-    for shift_y in range(3):
-        tap_row = []
-        for shift_x in range(3):
-            window = padded[:, shift_y : shift_y + height, shift_x : shift_x + width_cells]
-            tap_row.append(
-                lax.dot_general(
-                    upstream,
-                    window,
-                    (((1, 2), (1, 2)), ((), ())),
-                    preferred_element_type=jnp.float32,
-                )
-            )
-        tap_list.append(jnp.stack(tap_row, axis=-1))
-    return jnp.stack(tap_list, axis=-2)
-
-
-def flipped(kernel):
-    return jnp.transpose(kernel[:, :, ::-1, ::-1], (1, 0, 2, 3))
-
-
-def block_view(field):
-    channels, height, width_cells = field.shape
-    return field.astype(jnp.float32).reshape(channels, height // 2, 2, width_cells // 2, 2)
-
-
-def pooled(field):
-    return jnp.mean(block_view(field), axis=(2, 4)).astype(jnp.bfloat16)
-
-
-def block_sum(field):
-    return jnp.sum(block_view(field), axis=(2, 4)).astype(jnp.bfloat16)
-
-
-def upsampled(field):
-    return jnp.repeat(jnp.repeat(field, 2, axis=1), 2, axis=2)
-
-
-def gelu_back(preact, upstream):
-    return jax.vjp(jax.nn.gelu, preact)[1](upstream)[0]
-
-
-def fine_pad(field):
-    return with_halo(field, (("rows", 1), ("cols", 2)), 1)
-
-
-def coarse_pad(field):
-    return with_halo(field, (("rows", 1), ("cols", 2)), 1)
+def tap_major(kernel, order):
+    taps = jnp.transpose(kernel, (2, 3) + order)
+    return taps.reshape((9,) + taps.shape[2:])
 
 
 def body(level_input, kernel_a, kernel_b, kernel_c, kernel_d, cotangent):
-    padded_in = with_halo(level_input, (("rows", 1), ("cols", 2)), 1)
-    padded_cot = None
-    pre_a = conv_valid(padded_in, kernel_a)
-    hidden = jax.nn.gelu(pre_a).astype(jnp.bfloat16)
-    coarse = pooled(hidden)
-    padded_coarse = coarse_pad(coarse)
-    pre_b = conv_valid(padded_coarse, kernel_b)
-    middle = jax.nn.gelu(pre_b).astype(jnp.bfloat16)
-    padded_middle = coarse_pad(middle)
-    coarse_out = conv_valid(padded_middle, kernel_c).astype(jnp.bfloat16)
-    joined = (hidden.astype(jnp.float32) + upsampled(coarse_out).astype(jnp.float32)).astype(
-        jnp.bfloat16
-    )
-    padded_joined = fine_pad(joined)
-    result_field = conv_valid(padded_joined, kernel_d).astype(jnp.bfloat16)
-    padded_cot = with_halo(cotangent, (("rows", 1), ("cols", 2)), 1)
-    grad_joined = conv_valid(padded_cot, flipped(kernel_d)).astype(jnp.bfloat16)
-    sum_d = kernel_grad(padded_joined, cotangent)
-    grad_coarse = block_sum(grad_joined)
-    sum_c = kernel_grad(padded_middle, grad_coarse)
-    grad_pre_b = gelu_back(pre_b, conv_valid(coarse_pad(grad_coarse), flipped(kernel_c))).astype(
-        jnp.bfloat16
-    )
-    sum_b = kernel_grad(padded_coarse, grad_pre_b)
-    grad_pooled = conv_valid(coarse_pad(grad_pre_b), flipped(kernel_b)).astype(jnp.bfloat16)
-    grad_hidden = grad_joined.astype(jnp.float32) + 0.25 * upsampled(grad_pooled).astype(
-        jnp.float32
-    )
-    grad_pre_a = gelu_back(pre_a, grad_hidden).astype(jnp.bfloat16)
-    input_grad = conv_valid(fine_pad(grad_pre_a), flipped(kernel_a)).astype(jnp.bfloat16)
-    sum_a = kernel_grad(padded_in, grad_pre_a)
-    sums = (sum_a, sum_b, sum_c, sum_d)
-    flat = jnp.concatenate([s.reshape(-1, 128) for s in sums] + [jnp.zeros((320, 128), jnp.float32)])
-    flat = reduce_all(flat.reshape(128, 16, 128)).reshape(2048, 128)
-    start, totals = 0, []
-    for s in sums:
-        totals.append(flat[start : start + s.size // 128].reshape(s.shape))
-        start += s.size // 128
-    sum_a, sum_b, sum_c, sum_d = totals
+    row, col = lax.axis_index("rows"), lax.axis_index("cols")
+    last_row, last_col = lax.axis_size("rows") - 1, lax.axis_size("cols") - 1
+    edges = jnp.stack([row == 0, row == last_row, col == 0, col == last_col]).astype(jnp.int32)
+    rows, left, right = pack(level_input, cotangent)
+    above, below, from_left, from_right = exchange(rows, left, right)
+    result_field, input_grad, sums = levels(
+        edges, rows, above, below, from_left, from_right,
+        tap_major(kernel_a, (0, 1)), tap_major(kernel_b, (1, 0)),
+        tap_major(kernel_c, (0, 1)), tap_major(kernel_d, (0, 1)))
+    sums = reduce_all(sums.reshape(128, 16, 128)).reshape(2048, 128)
+    both = sums[0:576].reshape(3, 3, 64, 128)
+    grad_b = sums[576:1152].reshape(3, 3, 64, 128)
+    grad_c = sums[1152:1728].reshape(3, 3, 64, 128)
     total_cells = (
         level_input.shape[1] * level_input.shape[2] * lax.axis_size("rows") * lax.axis_size("cols")
     )
@@ -272,10 +549,10 @@
     return (
         result_field,
         input_grad,
-        sum_a * fine_scale,
-        sum_b * coarse_scale,
-        sum_c * coarse_scale,
-        sum_d * fine_scale,
+        jnp.transpose(both[..., :64] * fine_scale, (2, 3, 0, 1)),
+        jnp.transpose(grad_b * coarse_scale, (3, 2, 0, 1)),
+        jnp.transpose(grad_c * coarse_scale, (2, 3, 0, 1)),
+        jnp.transpose(both[..., 64:] * fine_scale, (2, 3, 0, 1)),
     )
 
 

time: 512 us -> 100 us (0.20); the launches traced: 504 us -> 99.9 us
  local copies, waits for them, and re-layouts: 174 us -> 1.93 us
  starting transfers between devices: 108 us -> 0 us
  waiting for transfers between devices: 61.3 us -> 0 us
  matrix products: 36.8 us -> 0 us
  Pallas kernels: 109 us -> 95.4 us
  other arithmetic: 12.2 us -> 1.87 us
    ppermute x32 -> x0, starting transfers between devices: 108 us -> none  [the longest x16 77.9 us: with_halo(): before = lax.ppermute(last, axis, up)]
    pallas_call x1, Pallas kernels: 109 us -> 40.3 us  [reduce_all(): pl.pallas_call(_reduce_kernel, out_shape=jax.ShapeDtypeStruct((128, 16, 1...]
    ppermute x32 -> x0, waiting for transfers between devices: 61.3 us -> none  [the longest x16 53.5 us: with_halo(): after = lax.ppermute(initial, axis, down)]
    pallas_call x0 -> x3, Pallas kernels: none -> 55.1 us  [the longest x1 29.2 us: exchange(): pl.pallas_call(_rim_kernel, out_shape=(shape(REACH), shape(REACH), shape(...]
    reshape x4 -> x0, local copies, waits for them, and re-layouts: 42.2 us -> none  [body(): s.reshape(-1, 128)]
    unnamed x85 -> x12, local copies, waits for them, and re-layouts: 43.7 us -> 1.93 us
    another operation x4 -> x0, local copies, waits for them, and re-layouts: 36.6 us -> none  [kernel_grad(): return jnp.stack(tap_list, axis=-2)]
    mul x6 -> x0, local copies, waits for them, and re-layouts: 34.7 us -> none  [the longest x1 10.9 us: body(): sum_c * coarse_scale]
  transfers between devices with their start and end apart: 32 -> 0, of which waited for: 5 -> 0; matrix products, arithmetic and copies ran while one was open for 22% -> 0% of each run, Pallas kernels for 22% -> 0%
where the time goes in v2:
time: 100 us; the launch traced here: 99.9 us
  Pallas kernels  95.4 us (95%)
  local copies, waits for them, and re-layouts  1.93 us (2%)
  other arithmetic  1.87 us (2%)
    pallas_call x1, Pallas kernels, reduce_all(): pl.pallas_call(_reduce_kernel, out_shape=jax.ShapeDtypeStruct((128, 16, 1...  40.3 us
    pallas_call x1, Pallas kernels, exchange(): pl.pallas_call(_rim_kernel, out_shape=(shape(REACH), shape(REACH), shape(...  29.2 us
    pallas_call x1, Pallas kernels, levels(): pl.pallas_call(_levels_kernel, out_shape=(jax.ShapeDtypeStruct((64, 16, 1...  25.4 us

profile of v2, /device:TPU:1, one launch (start us, length us, event | category | flops | bytes accessed | tf_op | source)
XLA Modules:
  0.0 99.9 jit_solution(9826402236108978870)
XLA Ops:
  0.6 0.1 add_convert_fusion.edge_ref
  0.7 0.0 copy-start
  0.7 0.9 copy-done
  1.7 0.0 copy-start.1
  1.7 0.9 copy-done.1
  2.6 0.5 shard_map.109
  3.1 0.0 copy-start.2
  3.1 0.0 copy-start.3
  3.2 0.0 copy-start.4
  3.2 0.0 copy-start.5
  3.2 29.2 %shard_map.110 = (bf16[7,128,128]{2,1,0:T(8,128)(2,1)S(1)}, bf16[7,128,128]{2,1,0:T(8,128)(2,1)S(1)}, bf16[3,128,128]{2,1,0:T(8,128)(2,1)S(1)}, bf16[3,128,128]{2,1,0:T(8,128)(2,1)S(1)}) custom-call(bf16[16,128,128]{2,1,0:T(8,128)(2,1)S(1)} %get-tuple-element.16.rows_ref, bf16[128,128]{1,0:T(8,128)(2,1)S(1)} %get-tuple-element.17.left_ref, ...), custom_call_target="tpu_custom_call" | custom-call | flops 1000 | bytes 2000000 | tf_op jit(solution)/shard_map/pallas_call | solution.py:82
  32.4 0.0 copy-done.2
  32.4 0.0 copy-done.3
  32.4 0.0 copy-done.4
  32.4 0.0 copy-done.5
  32.4 25.4 %shard_map.111 = (bf16[64,16,128]{2,1,0:T(8,128)(2,1)}, bf16[64,16,128]{2,1,0:T(8,128)(2,1)}, f32[2048,128]{1,0:T(8,128)S(1)}) custom-call(s32[4]{0:T(128)S(1)} %add_convert_fusion.edge_ref, bf16[16,128,128]{2,1,0:T(8,128)(2,1)S(1)} %get-tuple-element.16.rows_ref, bf16[7,128,128]{2,1,0:T(8,128)(2,1)S(1)} %get-tuple-element.19.above_ref, ...), custom_call_target="tpu_custom_call" | custom-call | flops 2000000000 | bytes 8000000 | tf_op jit(solution)/shard_map/pallas_call | solution.py:375
  57.9 40.3 %shard_map.112 = f32[128,16,128]{2,1,0:T(8,128)S(1)} custom-call(f32[128,16,128]{2,1,0:T(8,128)S(1)} %bitcast.28), custom_call_target="tpu_custom_call" | custom-call | flops 1000000 | bytes 4000000 | tf_op jit(solution)/shard_map/pallas_call | solution.py:502
  98.1 0.9 slice_multiply_fusion.2
  99.0 0.9 fusion
Async XLA Ops:
  0.7 1.0 copy-start
  1.7 0.9 copy-start.1
  3.1 29.3 %copy-start.2 = (bf16[64,64,3,3]{1,0,3,2:T(8,128)(2,1)S(1)}, bf16[64,64,3,3]{1,0,3,2:T(8,128)(2,1)}, u32[]{:S(2)}) copy-start(bf16[64,64,3,3]{1,0,3,2:T(8,128)(2,1)} %param.7) | copy-start | bytes 221188
  3.1 29.2 %copy-start.3 = (bf16[128,64,3,3]{0,1,3,2:T(8,128)(2,1)S(1)}, bf16[128,64,3,3]{0,1,3,2:T(8,128)(2,1)}, u32[]{:S(2)}) copy-start(bf16[128,64,3,3]{0,1,3,2:T(8,128)(2,1)} %param.8) | copy-start | bytes 442372
  3.2 29.2 %copy-start.4 = (bf16[64,128,3,3]{1,0,3,2:T(8,128)(2,1)S(1)}, bf16[64,128,3,3]{1,0,3,2:T(8,128)(2,1)}, u32[]{:S(2)}) copy-start(bf16[64,128,3,3]{1,0,3,2:T(8,128)(2,1)} %param.9) | copy-start | bytes 442372
  3.2 29.2 %copy-start.5 = (bf16[64,64,3,3]{1,0,3,2:T(8,128)(2,1)S(1)}, bf16[64,64,3,3]{1,0,3,2:T(8,128)(2,1)}, u32[]{:S(2)}) copy-start(bf16[64,64,3,3]{1,0,3,2:T(8,128)(2,1)} %param.10) | copy-start | bytes 221188

commit v3 on v0

v3 whole, which is shorter than its diff:
```python
import functools
import math

import jax
import jax.numpy as jnp
from jax import lax
from jax.experimental import pallas as pl
from jax.experimental.pallas import tpu as pltpu
from jax.sharding import PartitionSpec as P

MESH = pl.DeviceIdType.MESH
BF, F32 = jnp.bfloat16, jnp.float32
VMEM = pl.BlockSpec(memory_space=pltpu.VMEM)
GELU_SCALE = 0.7978845608028654
GELU_CUBE = 0.044715
REACH = 7


def _gelu_parts(x):
    square = x * x
    bend = jnp.tanh(GELU_SCALE * (x + GELU_CUBE * (x * square)))
    half = 0.5 + 0.5 * bend
    slope = half + (0.5 * GELU_SCALE) * x * (1.0 - bend * bend) * (1.0 + (3.0 * GELU_CUBE) * square)
    return x * half, slope


def _taps(x):
    lanes = x.shape[1]
    return jnp.concatenate(
        [pltpu.roll(x, 1, axis=1).astype(BF), x.astype(BF), pltpu.roll(x, lanes - 1, axis=1).astype(BF)],
        axis=0)


def _dot(a, b):
    return jnp.dot(a, b, preferred_element_type=F32)


def _dot_t(a, b):
    return lax.dot_general(a, b, (((1,), (1,)), ((), ())), preferred_element_type=F32)


def _loop(first, last, step, unroll=1):
    def body(i, carry):
        step(i)
        return carry
    lax.fori_loop(first, last, body, 0, unroll=unroll)


class _Sum:
    def __init__(self, whole, src, *rest):
        self.whole, self.src, self.sems = whole, src, rest[6:]
        (self.pair_out, self.pair_in, self.plane_out, self.plane_in, self.near_all, self.far_all) = rest[:6]
        self.half = src.shape[0] // 2
        self.piece, self.chunk = self.half // 4, self.half // 16
        rows, cols = lax.axis_index("rows"), lax.axis_index("cols")
        self.y, self.near, self.core = rows // 8, (rows // 2) % 4, rows % 2
        self.far_at, self.x = cols // 4, cols % 4
        self.partner = self.place(1 - self.core, 0, 0, 0, 0)
        self.steps = [(dy, dx) for dy in (2, 1, 3, 0) for dx in (2, 1, 3, 0)]
        self.base = self.core * self.half + self.y * self.piece + self.x * self.chunk
        self.started = []

    def place(self, core, dy, dx, dn, df):
        return (((self.y + dy) % 4) * 8 + ((self.near + dn) % 4) * 2 + core,
                ((self.far_at + df) % 4) * 4 + (self.x + dx) % 4)

    def peers(self):
        found = [self.partner]
        found += [self.place(self.core, dy, dx, 0, 0) for dy, dx in self.steps if (dy, dx) != (0, 0)]
        found += [self.place(self.core, 0, 0, d, 0) for d in (1, 2, 3)]
        found += [self.place(self.core, 0, 0, 0, d) for d in (1, 2, 3)]
        return found

    def send(self, src, dst, phase, k, peer):
        copy = pltpu.make_async_remote_copy(
            src_ref=src, dst_ref=dst, send_sem=self.sems[2 * phase].at[k],
            recv_sem=self.sems[2 * phase + 1].at[k], device_id=peer, device_id_type=MESH)
        copy.start()
        self.started.append(copy)
        return copy

    def pair(self):
        self.copies = {}
        theirs = (1 - self.core) * self.half
        for dy in (2, 1, 3, 0):
            first = ((self.y + dy) % 4) * self.piece
            piece = pl.ds(first, self.piece)
            self.pair_out[piece] = self.src[pl.ds(theirs + first, self.piece)].astype(BF)
            self.copies[dy] = self.send(
                self.pair_out.at[piece], self.pair_in.at[piece], 0, dy, self.partner)

    def plane(self):
        mine, pair, self.copies = self.core * self.half, self.copies, {}
        for dy, dx in self.steps:
            if dx == 2:
                pair[dy].wait_recv()
            first = ((self.y + dy) % 4) * self.piece + ((self.x + dx) % 4) * self.chunk
            chunk = pl.ds(first, self.chunk)
            both = self.src[pl.ds(mine + first, self.chunk)] + self.pair_in[chunk].astype(F32)
            if (dy, dx) == (0, 0):
                self.own = both
            else:
                k = dy * 4 + dx
                self.plane_out[chunk] = both.astype(BF)
                self.copies[k] = self.send(
                    self.plane_out.at[chunk], self.plane_in.at[k], 1, k,
                    self.place(self.core, dy, dx, 0, 0))

    def along_near(self):
        total = self.own
        for k in (4, 12, 1, 3, 8, 2, 5, 7, 13, 15, 6, 14, 9, 11, 10):
            self.copies[k].wait_recv()
            total = total + self.plane_in[k].astype(F32)
        self.near_all[self.near] = total
        at = self.near_all.at[self.near]
        self.copies = {}
        for d in (2, 1, 3):
            self.copies[d] = self.send(at, at, 2, d, self.place(self.core, 0, 0, d, 0))

    def along_far(self):
        for d in (1, 3, 2):
            self.copies[d].wait_recv()
        near = self.near_all
        self.far_all[self.far_at] = ((near[0] + near[1]) + near[2]) + near[3]
        at = self.far_all.at[self.far_at]
        self.copies = {}
        for d in (2, 1, 3):
            self.copies[d] = self.send(at, at, 3, d, self.place(self.core, 0, 0, 0, d))

    def back_plane(self):
        for d in (1, 3, 2):
            self.copies[d].wait_recv()
        far, chunk = self.far_all, pl.ds(self.base, self.chunk)
        self.whole[chunk] = (((far[0] + far[1]) + far[2]) + far[3]).astype(BF)
        at = self.whole.at[chunk]
        self.copies = {}
        for dy, dx in self.steps:
            if (dy, dx) != (0, 0):
                k = dy * 4 + dx
                self.copies[k] = self.send(at, at, 4, k, self.place(self.core, dy, dx, 0, 0))

    def back_pair(self):
        plane, self.copies = self.copies, {}
        for dy in (0, 1, 3, 2):
            for dx in (0, 1, 3, 2):
                if (dy, dx) != (0, 0):
                    plane[dy * 4 + dx].wait_recv()
            first = self.core * self.half + ((self.y - dy + 4) % 4) * self.piece
            at = self.whole.at[pl.ds(first, self.piece)]
            self.copies[dy] = self.send(at, at, 5, dy, self.partner)

    def finish(self):
        for dy in (0, 1, 3, 2):
            self.copies[dy].wait_recv()
        for copy in self.started:
            copy.wait_send()


def _levels_kernel(x_at, cot_at, ka_at, kb_at, kc_at, kd_at,
                   result_ref, input_grad_ref, early_out, late_out,
                   x_ref, cot_ref, ka_ref, kb_ref, kc_ref, kd_ref,
                   rows_ref, left_ref, right_ref, above_ref, below_ref, from_left_ref, from_right_ref,
                   up_corners, down_corners, above_corners, below_corners,
                   wa, wat, wb, wbt, wc, wct, wd, wdt, pool, spread,
                   x3, cot3, parts, cot_parts, cparts, hidden, slope_a, slope_b, coarse3, middle3,
                   coarse_out, joined3, grad_joined, grad_coarse3, grad_b3, grad_pool, up, grad_a3,
                   pad_a, pad_b, pad_c, pad_d, flat, acc, *rest):
    load_sem, rim_send, rim_recv = rest[:3]
    early_rest, late_rest = rest[3:23], rest[23:43]
    row, col = lax.axis_index("rows"), lax.axis_index("cols")
    height, width = lax.axis_size("rows"), lax.axis_size("cols")
    top = (row == 0).astype(jnp.int32)
    bottom = (row == height - 1).astype(jnp.int32)
    low = (col == 0).astype(jnp.int32)
    high = (col == width - 1).astype(jnp.int32)

    early, late = _Sum(*early_rest), _Sum(*late_rest)
    early_src, late_src = early.src, late.src

    def beside(dr, dc):
        return ((row + dr + height) % height, (col + dc + width) % width)

    around = [(0, -1), (0, 1), (-1, 0), (1, 0)]
    greeted = [beside(dr, dc) for dr, dc in around] + early.peers()
    barrier = pltpu.get_barrier_semaphore()
    for peer in greeted:
        pl.semaphore_signal(barrier, inc=1, device_id=peer, device_id_type=MESH)
    loads = [
        pltpu.make_async_copy(src, dst, load_sem.at[k]) for k, (src, dst) in enumerate((
            (x_at, x_ref), (cot_at, cot_ref), (ka_at, ka_ref), (kb_at, kb_ref), (kc_at, kc_ref), (kd_at, kd_ref)))]
    for load in loads:
        load.start()

    lane = lax.broadcasted_iota(jnp.int32, (64, 128), 1) // 8
    for field, ref in ((0, x_ref), (1, cot_ref)):
        loads[field].wait()
        flat[...] = ref[...].astype(F32).reshape(1024, 128)
        at = pl.ds(field * 64, 64)
        left = jnp.zeros((64, 128), F32)
        right = jnp.zeros((64, 128), F32)
        for h in range(16):
            line = flat[pl.ds(h, 64, stride=16), :]
            rows_ref[h, at, :] = line.astype(BF)
            left = jnp.where(lane == h, line if h == 0 else pltpu.roll(line, 8 * h, axis=1), left)
            right = jnp.where(lane == h, line if h == 15 else pltpu.roll(line, 8 * h + 8, axis=1), right)
        left_ref[at, :] = left.astype(BF)
        right_ref[at, :] = right.astype(BF)
    pl.semaphore_wait(barrier, len(greeted))
    rim = []

    def push(src, dst, offset):
        rim.append(pltpu.make_async_remote_copy(
            src_ref=src, dst_ref=dst, send_sem=rim_send.at[len(rim)], recv_sem=rim_recv.at[len(rim)],
            device_id=beside(*offset), device_id_type=MESH))
        rim[-1].start()

    push(left_ref, from_right_ref, (0, -1))
    push(right_ref, from_left_ref, (0, 1))
    push(rows_ref.at[pl.ds(0, REACH)], below_ref, (-1, 0))
    push(rows_ref.at[pl.ds(16 - REACH, REACH)], above_ref, (1, 0))
    f_lane = lax.broadcasted_iota(jnp.int32, (1, 256), 1)
    c_lane = lax.broadcasted_iota(jnp.int32, (1, 128), 1)
    f_mask = ((f_lane < 136 - 8 * high) | (f_lane >= 248 + 8 * low)).astype(F32)
    c_mask = ((c_lane < 68 - 4 * high) | (c_lane >= 124 + 4 * low)).astype(F32)
    own_c = (c_lane < 64).astype(F32)

    for load in loads[2:]:
        load.wait()
    for a in range(3):
        for b in range(3):
            tap, flip = 3 * a + b, 8 - (3 * a + b)
            at64, at128 = pl.ds(64 * a, 64), pl.ds(128 * a, 128)
            col64, col128 = slice(64 * b, 64 * b + 64), slice(128 * b, 128 * b + 128)
            wa[at64, col64] = ka_ref[tap]
            wd[at64, col64] = kd_ref[tap]
            wc[at64, col128] = kc_ref[tap]
            wbt[at64, col128] = kb_ref[flip]
            wat[at64, col64] = ka_ref[flip].astype(F32).T.astype(BF)
            wdt[at64, col64] = kd_ref[flip].astype(F32).T.astype(BF)
            wb[at128, col64] = kb_ref[tap].astype(F32).T.astype(BF)
            wct[at128, col64] = kc_ref[flip].astype(F32).T.astype(BF)
    cell = lax.broadcasted_iota(jnp.int32, (512, 128), 0)
    block = lax.broadcasted_iota(jnp.int32, (512, 128), 1)
    pool[...] = ((cell % 256) // 2 == block).astype(F32).astype(BF)
    cell = lax.broadcasted_iota(jnp.int32, (128, 256), 1)
    block = lax.broadcasted_iota(jnp.int32, (128, 256), 0)
    spread[...] = (cell // 2 == block).astype(F32).astype(BF)

    side_lane = lax.broadcasted_iota(jnp.int32, (128, 128), 1)

    def unpack(i):
        h = i - REACH
        if h < 0:
            center, left, right, p = above_ref[h + REACH], above_corners[...], above_corners[...], h + 16
            turn_left, turn_right = (184 - 8 * p) % 128, 128 - 8 * p
        elif h < 16:
            center, left, right, p = rows_ref[h], from_left_ref[...], from_right_ref[...], h
            turn_left, turn_right = 120 - 8 * p, (128 - 8 * p) % 128
        else:
            center, left, right, p = below_ref[h - 16], below_corners[...], below_corners[...], h - 16
            turn_left, turn_right = 120 - 8 * p, 64 - 8 * p
        left, right = left.astype(F32), right.astype(F32)
        right = pltpu.roll(right, turn_right, axis=1) if turn_right else right
        left = pltpu.roll(left, turn_left, axis=1) if turn_left else left
        side = jnp.where(side_lane < 8, right, left)
        wide = jnp.concatenate([center.astype(F32), side], axis=1) * f_mask
        x3[i] = _taps(wide[:64])
        cot3[i] = _taps(wide[64:])

    def conv(weights, source, into, first, last, unroll):
        def step(i):
            into[i] = _dot(weights[...], source[i])
        _loop(first, last, step, unroll)

    rim[0].wait_recv()
    rim[1].wait_recv()
    left, right = from_left_ref[...].astype(F32), from_right_ref[...].astype(F32)
    up_corners[...] = jnp.where(side_lane < 64, left, pltpu.roll(right, 64, axis=1)).astype(BF)
    down_corners[...] = jnp.where(side_lane < 64, pltpu.roll(left, 64, axis=1), right).astype(BF)
    push(up_corners, below_corners, (-1, 0))
    push(down_corners, above_corners, (1, 0))
    for i in range(REACH, REACH + 16):
        unpack(i)
    conv(wa, x3, parts, 7, 23, 4)
    conv(wdt, cot3, cot_parts, 7, 23, 4)
    for copy in rim[2:]:
        copy.wait_recv()
    for i in list(range(REACH)) + list(range(REACH + 16, 30)):
        unpack(i)

    def clear(ref, top_rows, total):
        @pl.when(top == 1)
        def _():
            ref[pl.ds(0, top_rows)] = jnp.zeros((top_rows,) + ref.shape[1:], ref.dtype)

        @pl.when(bottom == 1)
        def _():
            ref[pl.ds(total - top_rows, top_rows)] = jnp.zeros((top_rows,) + ref.shape[1:], ref.dtype)

    clear(x3, 7, 30)
    clear(cot3, 7, 30)

    def gathered(from_, i, outs):
        return from_[i - 1, 0:outs] + from_[i, outs:2 * outs] + from_[i + 1, 2 * outs:3 * outs]

    for first_row in (0, 23):
        conv(wa, x3, parts, first_row, first_row + 7, 7)
        conv(wdt, cot3, cot_parts, first_row, first_row + 7, 7)

    def first(with_slope):
        def step(k):
            for s in range(2):
                pre = gathered(parts, 2 * k + 1 + s, 64)
                value, slope = _gelu_parts(pre)
                hidden[k, :, 256 * s:256 * s + 256] = (value * f_mask).astype(BF)
                if with_slope:
                    slope_a[k - 2, :, 256 * s:256 * s + 256] = slope
        return step
    _loop(0, 2, first(False))
    _loop(2, 12, first(True))
    _loop(12, 14, first(False))
    clear(hidden, 3, 14)

    def pool_step(k):
        coarse3[k] = _taps((_dot(hidden[k], pool[...]) * 0.25).astype(BF).astype(F32))
    _loop(0, 14, pool_step, 7)

    conv(wb, coarse3, cparts, 0, 14, 7)

    def second(k):
        value, slope = _gelu_parts(gathered(cparts, k + 1, 128))
        middle3[k] = _taps(value * c_mask)
        slope_b[k] = slope
    _loop(0, 12, second, 2)
    clear(middle3, 2, 12)

    def third(k):
        cparts[k, 0:192] = _dot(wc[...], middle3[k])
    _loop(0, 12, third, 6)

    def third_sum(k):
        coarse_out[k] = (gathered(cparts, k + 1, 64) * c_mask).astype(BF)
    _loop(0, 10, third_sum, 5)
    clear(coarse_out, 1, 10)

    def spread_step(source):
        def step(k):
            up[k] = _dot(source[k], spread[...])
        return step
    _loop(0, 10, spread_step(coarse_out), 5)

    def join(k, s):
        both = hidden[k + 2, :, 256 * s:256 * s + 256].astype(F32) + up[k]
        joined3[2 * k - 1 + s] = _taps(both)[:, 0:128]
    join(0, 1)

    def join_step(k):
        join(k, 0)
        join(k, 1)
    _loop(1, 9, join_step, 2)
    join(9, 0)

    def out_parts(weights, source):
        def step(i):
            parts[i, :, 0:128] = _dot(weights[...], source[i])
        _loop(0, 18, step, 6)

    def out_rows(ref):
        for h in range(16):
            flat[pl.ds(h, 64, stride=16), :] = gathered(
                parts.at[:, :, pl.ds(0, 128)], h + 1, 64)
        ref[...] = flat[...].reshape(64, 16, 128).astype(BF)

    out_parts(wd, joined3)
    out_rows(result_ref)

    def stacked(pad, j):
        return jnp.concatenate([pad[j + 2], pad[j + 1], pad[j]], axis=0)

    def pair(one, j):
        return jnp.concatenate([one(2 * j), one(2 * j + 1)], axis=1)

    def framed(pad, first, count, own):
        pad[pl.ds(0, 2)] = jnp.zeros((2,) + pad.shape[1:], BF)
        pad[pl.ds(count + 2, 2)] = jnp.zeros((2,) + pad.shape[1:], BF)

        def step(h):
            pad[h + 2] = own(h + first)
        _loop(0, count, step, 4)

    def fine_weight_grad(pad, window, src, first):
        acc[0:192, 0:192] = jnp.zeros((192, 192), F32)

        def step(j):
            acc[0:192, 0:192] += _dot_t(pair(lambda i: stacked(pad, i), j), pair(window, j))
        _loop(0, 9, step, 3)

        def tap(t):
            if t > 8:
                return jnp.zeros((64, 64), F32)
            a, b = t // 3, t % 3
            return acc[64 * a:64 * a + 64, 64 * b:64 * b + 64]
        for t in range(5):
            both = jnp.concatenate([tap(t), tap(t + 5)], axis=1)
            src[pl.ds(first + 4 * t, 4)] = both.reshape(4, 16, 128)

    framed(pad_d, 7, 16, lambda h: cot3[h, 64:128, 0:128])
    fine_weight_grad(pad_d, lambda i: joined3[i], early_src, 36)


    def back_first(k):
        for s in range(2):
            grad = gathered(cot_parts, 2 * k + 1 + s, 64) * f_mask
            grad_joined[k, :, 256 * s:256 * s + 256] = grad.astype(BF)
    _loop(0, 14, back_first, 2)
    clear(grad_joined, 3, 14)

    def back_pool(k):
        grad_coarse3[k] = _taps(_dot(grad_joined[k], pool[...]).astype(BF).astype(F32))
    _loop(0, 14, back_pool, 7)

    framed(pad_c, 3, 8, lambda k: (grad_coarse3[k, 64:128, :].astype(F32) * own_c).astype(BF))
    acc[0:192, 0:384] = jnp.zeros((192, 384), F32)

    def c_step(j):
        acc[0:192, 0:384] += _dot_t(
            pair(lambda i: stacked(pad_c, i), j), pair(lambda i: middle3[i + 1], j))
    _loop(0, 5, c_step, 1)
    for a in range(3):
        for b in range(3):
            early_src[pl.ds(4 * (3 * a + b), 4)] = acc[
                64 * a:64 * a + 64, 128 * b:128 * b + 128].reshape(4, 16, 128)
    conv(wct, grad_coarse3, cparts, 0, 14, 7)

    def back_second(k):
        grad_b3[k] = _taps(slope_b[k] * gathered(cparts, k + 1, 128) * c_mask)
    _loop(0, 12, back_second, 2)
    clear(grad_b3, 2, 12)

    def b_own(k):
        pad_b[k] = (grad_b3[k + 2, 128:256, :].astype(F32) * own_c).astype(BF)
    _loop(0, 8, b_own, 4)

    def b_window(k):
        return jnp.concatenate([coarse3[k + 2], coarse3[k + 3], coarse3[k + 4]], axis=0)
    early_src[pl.ds(56, 36)] = jnp.zeros((36, 16, 128), F32)
    early_src[pl.ds(92, 4)] = jnp.zeros((4, 16, 128), F32)

    def b_step(j):
        early_src[pl.ds(56, 36)] += _dot_t(
            pair(b_window, j), pair(lambda k: pad_b[k], j)).reshape(36, 16, 128)
    _loop(0, 4, b_step, 2)
    early.pair()

    def back_third(k):
        cparts[k, 0:192] = _dot(wbt[...], grad_b3[k])
    _loop(0, 12, back_third, 6)

    def back_third_sum(k):
        grad_pool[k] = gathered(cparts, k + 1, 64).astype(BF)
    _loop(0, 10, back_third_sum, 5)
    _loop(0, 10, spread_step(grad_pool), 5)

    def back_join(k, s):
        at = slice(256 * s, 256 * s + 256)
        grad = grad_joined[k + 2, :, at].astype(F32) + 0.25 * up[k]
        grad_a3[2 * k - 1 + s] = _taps(slope_a[k, :, at] * grad * f_mask)[:, 0:128]
    early.plane()
    back_join(0, 1)

    def back_join_step(k):
        back_join(k, 0)
        back_join(k, 1)
    _loop(1, 9, back_join_step, 2)
    back_join(9, 0)
    clear(grad_a3, 1, 18)
    early.along_near()
    framed(pad_a, 1, 16, lambda h: grad_a3[h, 64:128, :])
    late_src[pl.ds(20, 12)] = jnp.zeros((12, 16, 128), F32)
    fine_weight_grad(pad_a, lambda i: x3[i + 6, :, 0:128], late_src, 0)
    late.pair()
    early.along_far()
    out_parts(wat, grad_a3)
    late.plane()
    out_rows(input_grad_ref)
    late.along_near()
    early.back_plane()
    late.along_far()
    early.back_pair()
    late.back_plane()
    early.finish()
    early_out[...] = early.whole[...]
    late.back_pair()
    late.finish()
    late_out[...] = late.whole[...]
    for copy in rim:
        copy.wait_send()


def _sum_scratch(tiles):
    half, chunk = tiles // 2, tiles // 32
    buffers = [
        ((tiles, 16, 128), BF), ((tiles, 16, 128), F32),
        ((half, 16, 128), BF), ((half, 16, 128), BF), ((half, 16, 128), BF),
        ((16, chunk, 16, 128), BF), ((4, chunk, 16, 128), F32), ((4, chunk, 16, 128), F32),
    ]
    sems = [pltpu.SemaphoreType.DMA((count,)) for count in (4, 4, 16, 16, 4, 4, 4, 4, 16, 16, 4, 4)]
    return [pltpu.VMEM(shape, dtype) for shape, dtype in buffers] + sems


def levels(level_input, cotangent, ka, kb, kc, kd):
    scratch = [
        ((64, 16, 128), BF), ((64, 16, 128), BF),
        ((9, 64, 64), BF), ((9, 64, 128), BF), ((9, 64, 128), BF), ((9, 64, 64), BF),
        ((16, 128, 128), BF), ((128, 128), BF), ((128, 128), BF),
        ((REACH, 128, 128), BF), ((REACH, 128, 128), BF), ((128, 128), BF), ((128, 128), BF),
        ((128, 128), BF), ((128, 128), BF), ((128, 128), BF), ((128, 128), BF),
        ((192, 192), BF), ((192, 192), BF), ((384, 192), BF), ((192, 384), BF),
        ((192, 384), BF), ((384, 192), BF), ((192, 192), BF), ((192, 192), BF),
        ((512, 128), BF), ((128, 256), BF),
        ((30, 192, 256), BF), ((30, 192, 256), BF), ((30, 192, 256), F32), ((30, 192, 256), F32),
        ((14, 384, 128), F32),
        ((14, 64, 512), BF), ((10, 64, 512), F32), ((12, 128, 128), F32),
        ((14, 192, 128), BF), ((12, 384, 128), BF), ((10, 64, 128), BF),
        ((18, 192, 128), BF), ((14, 64, 512), BF), ((14, 192, 128), BF), ((12, 384, 128), BF),
        ((10, 64, 128), BF), ((10, 64, 256), F32), ((18, 192, 128), BF),
        ((20, 64, 128), BF), ((8, 128, 128), BF), ((12, 64, 128), BF), ((20, 64, 128), BF),
        ((1024, 128), F32), ((192, 512), F32),
    ]
    dma = pltpu.SemaphoreType.DMA
    out = lambda shape, dtype: jax.ShapeDtypeStruct(shape, dtype)
    return pl.pallas_call(
        _levels_kernel,
        out_shape=(
            out((64, 16, 128), BF), out((64, 16, 128), BF), out((96, 16, 128), BF), out((32, 16, 128), BF)),
        in_specs=[pl.BlockSpec(memory_space=pltpu.HBM)] * 6,
        out_specs=(VMEM,) * 4,
        scratch_shapes=[pltpu.VMEM(shape, dtype) for shape, dtype in scratch]
        + [dma((6,)), dma((6,)), dma((6,))] + _sum_scratch(96) + _sum_scratch(32),
        compiler_params=pltpu.CompilerParams(
            collective_id=0, has_side_effects=True, vmem_limit_bytes=60 * 1024 * 1024),
        cost_estimate=pl.CostEstimate(flops=2000000000, bytes_accessed=8000000, transcendentals=1000000),
    )(level_input, cotangent, ka, kb, kc, kd)


def _finish_kernel(fine_scale, coarse_scale, result_in, input_grad_in, early_ref, late_ref,
                   result_ref, input_grad_ref, grad_a_ref, grad_b_ref, grad_c_ref, grad_d_ref):
    result_ref[...] = result_in[...]
    input_grad_ref[...] = input_grad_in[...]
    grad_c_ref[...] = early_ref[pl.ds(0, 36)].astype(F32).reshape(9, 64, 128) * coarse_scale
    grad_b_ref[...] = early_ref[pl.ds(56, 36)].astype(F32).reshape(9, 64, 128) * coarse_scale
    for ref, taps in ((grad_d_ref, early_ref[pl.ds(36, 20)]), (grad_a_ref, late_ref[pl.ds(0, 20)])):
        fine = taps.astype(F32).reshape(5, 64, 128) * fine_scale
        ref[pl.ds(0, 5)] = fine[:, :, 0:64]
        ref[pl.ds(5, 4)] = fine[0:4, :, 64:128]


def finish(result, input_grad, early, late, fine_scale, coarse_scale):
    out = lambda shape, dtype: jax.ShapeDtypeStruct(shape, dtype)
    return pl.pallas_call(
        functools.partial(_finish_kernel, fine_scale, coarse_scale),
        out_shape=(
            out((64, 16, 128), BF), out((64, 16, 128), BF), out((9, 64, 64), F32),
            out((9, 64, 128), F32), out((9, 64, 128), F32), out((9, 64, 64), F32)),
        in_specs=[VMEM] * 4,
        out_specs=(VMEM,) * 6,
        compiler_params=pltpu.CompilerParams(vmem_limit_bytes=8 * 1024 * 1024),
        cost_estimate=pl.CostEstimate(flops=1000000, bytes_accessed=2000000, transcendentals=0),
    )(result, input_grad, early, late)


def tap_major(kernel, order):
    taps = jnp.transpose(kernel, (2, 3) + order)
    return taps.reshape((9,) + taps.shape[2:])


def from_taps(grad, order):
    return jnp.transpose(grad.reshape((3, 3) + grad.shape[1:]), order)


def body(level_input, kernel_a, kernel_b, kernel_c, kernel_d, cotangent):
    total_cells = (
        level_input.shape[1] * level_input.shape[2] * lax.axis_size("rows") * lax.axis_size("cols")
    )
    parts = levels(
        level_input, cotangent,
        tap_major(kernel_a, (0, 1)), tap_major(kernel_b, (1, 0)),
        tap_major(kernel_c, (0, 1)), tap_major(kernel_d, (0, 1)))
    result_field, input_grad, grad_a, grad_b, grad_c, grad_d = finish(
        *parts, 1.0 / math.sqrt(total_cells), 1.0 / math.sqrt(total_cells // 4))
    return (
        result_field,
        input_grad,
        from_taps(grad_a, (2, 3, 0, 1)),
        from_taps(grad_b, (3, 2, 0, 1)),
        from_taps(grad_c, (2, 3, 0, 1)),
        from_taps(grad_d, (2, 3, 0, 1)),
    )


def solution(mesh):
    placed = (P(None, "rows", "cols"), P(), P(), P(), P(), P(None, "rows", "cols"))
    return jax.shard_map(
        body,
        mesh=mesh,
        in_specs=placed,
        out_specs=(P(None, "rows", "cols"), P(None, "rows", "cols"), P(), P(), P(), P()),
        check_vma=False,
    )
```

time: 774 us -> 85 us (0.11)
  waiting for transfers between devices: 602 us -> 0 us
  starting transfers between devices: 101 us -> 0 us
  Pallas kernels: 0 us -> 80.3 us
  matrix products: 19.6 us -> 0 us
  other arithmetic: 15.7 us -> 0 us
  between operations: 15.7 us -> 0.65 us
  local copies, waits for them, and re-layouts: 18.4 us -> 3.79 us
    psum x1 -> x0, waiting for transfers between devices: 520 us -> none  [body(): lax.psum((sum_a, sum_b, sum_c, sum_d), ('rows', 'cols'))]
    ppermute x32 -> x0, starting transfers between devices: 101 us -> none  [the longest x16 71.7 us: with_halo(): before = lax.ppermute(last, axis, up)]
    ppermute x32 -> x0, waiting for transfers between devices: 81.6 us -> none  [the longest x16 76.7 us: with_halo(): after = lax.ppermute(initial, axis, down)]
    pallas_call x0 -> x2, Pallas kernels: none -> 80.3 us  [the longest x1 79 us: levels(): pl.pallas_call(_levels_kernel, out_shape=(out((64, 16, 128), BF), out((64...]
    dot_general x36 -> x0, matrix products: 13 us -> none  [kernel_grad(): lax.dot_general(upstream, window, (((1, 2), (1, 2)), ((), ())), preferred...]
  transfers between devices with their start and end apart: 33 -> 0, of which waited for: 10 -> 0; matrix products, arithmetic and copies ran while one was open for 4% -> 0% of each run, Pallas kernels for 0% -> 0%
where the time goes in v3:
time: 85 us; the launch traced here: 84.7 us
  Pallas kernels  80.3 us (94%)
  local copies, waits for them, and re-layouts  3.79 us (4%)
    pallas_call x1, Pallas kernels, levels(): pl.pallas_call(_levels_kernel, out_shape=(out((64, 16, 128), BF), out((64...  79 us
    unnamed x8, local copies, waits for them, and re-layouts  3.79 us

profile of v3, /device:TPU:1, one launch (start us, length us, event | category | flops | bytes accessed | tf_op | source)
XLA Modules:
  0.0 84.7 jit_solution(2148866902954698912)
XLA Ops:
  0.6 79.0 %shard_map.109 = (bf16[64,16,128]{2,1,0:T(8,128)(2,1)}, bf16[64,16,128]{2,1,0:T(8,128)(2,1)}, bf16[96,16,128]{2,1,0:T(8,128)(2,1)}, bf16[32,16,128]{2,1,0:T(8,128)(2,1)}) custom-call(bf16[64,16,128]{2,1,0:T(8,128)(2,1)} %x_at.1, bf16[64,16,128]{2,1,0:T(8,128)(2,1)} %cot_at.1, bf16[9,64,64]{2,1,0:T(8,128)(2,1)} %bitcast.28, bf16[9,64,128]{2,1,0:T(8,128)(2,1)} %bitcast.29, ...), custom_call_target="tpu_custom_call" | custom-call | flops 2000000000 | bytes 8000000 | tf_op jit(solution)/shard_map/pallas_call | solution.py:532
  79.7 0.0 copy-start
  79.7 1.0 %copy-done = bf16[96,16,128]{2,1,0:T(8,128)(2,1)S(1)} copy-done((bf16[96,16,128]{2,1,0:T(8,128)(2,1)S(1)}, bf16[96,16,128]{2,1,0:T(8,128)(2,1)}, u32[]{:S(2)}) %copy-start) | copy-done | bytes 393240
  80.7 0.0 copy-start.1
  80.7 0.9 %copy-done.1 = bf16[64,16,128]{2,1,0:T(8,128)(2,1)S(1)} copy-done((bf16[64,16,128]{2,1,0:T(8,128)(2,1)S(1)}, bf16[64,16,128]{2,1,0:T(8,128)(2,1)}, u32[]{:S(2)}) %copy-start.1) | copy-done | bytes 262168
  81.6 0.0 copy-start.2
  81.6 0.9 %copy-done.2 = bf16[64,16,128]{2,1,0:T(8,128)(2,1)S(1)} copy-done((bf16[64,16,128]{2,1,0:T(8,128)(2,1)S(1)}, bf16[64,16,128]{2,1,0:T(8,128)(2,1)}, u32[]{:S(2)}) %copy-start.2) | copy-done | bytes 262168
  82.6 0.0 copy-start.3
  82.6 0.9 %copy-done.3 = bf16[32,16,128]{2,1,0:T(8,128)(2,1)S(1)} copy-done((bf16[32,16,128]{2,1,0:T(8,128)(2,1)S(1)}, bf16[32,16,128]{2,1,0:T(8,128)(2,1)}, u32[]{:S(2)}) %copy-start.3) | copy-done | bytes 131096
  83.5 1.3 %shard_map.110 = (bf16[64,16,128]{2,1,0:T(8,128)(2,1)}, bf16[64,16,128]{2,1,0:T(8,128)(2,1)}, f32[9,64,64]{2,1,0:T(8,128)}, f32[9,64,128]{2,1,0:T(8,128)}, f32[9,64,128]{2,1,0:T(8,128)}, /*index=5*/f32[9,64,64]{2,1,0:T(8,128)}) custom-call(bf16[64,16,128]{2,1,0:T(8,128)(2,1)S(1)} %copy-done.1, bf16[64,16,128]{2,1,0:T(8,128)(2,1)S(1)} %copy-done.2, ...), custom_call_target="tpu_custom_call" | custom-call | flops 1000000 | bytes 2000000 | tf_op jit(solution)/shard_map/pallas_call | solution.py:560
Async XLA Ops:
  79.7 1.0 %copy-start = (bf16[96,16,128]{2,1,0:T(8,128)(2,1)S(1)}, bf16[96,16,128]{2,1,0:T(8,128)(2,1)}, u32[]{:S(2)}) copy-start(bf16[96,16,128]{2,1,0:T(8,128)(2,1)} %get-tuple-element.18.early_ref) | copy-start | bytes 1179652
  80.7 0.9 %copy-start.1 = (bf16[64,16,128]{2,1,0:T(8,128)(2,1)S(1)}, bf16[64,16,128]{2,1,0:T(8,128)(2,1)}, u32[]{:S(2)}) copy-start(bf16[64,16,128]{2,1,0:T(8,128)(2,1)} %get-tuple-element.16.result_in) | copy-start | bytes 786436
  81.6 0.9 %copy-start.2 = (bf16[64,16,128]{2,1,0:T(8,128)(2,1)S(1)}, bf16[64,16,128]{2,1,0:T(8,128)(2,1)}, u32[]{:S(2)}) copy-start(bf16[64,16,128]{2,1,0:T(8,128)(2,1)} %get-tuple-element.17.input_grad_in) | copy-start | bytes 786436
  82.6 0.9 %copy-start.3 = (bf16[32,16,128]{2,1,0:T(8,128)(2,1)S(1)}, bf16[32,16,128]{2,1,0:T(8,128)(2,1)}, u32[]{:S(2)}) copy-start(bf16[32,16,128]{2,1,0:T(8,128)(2,1)} %get-tuple-element.19.late_ref) | copy-start | bytes 393220

commit v4 on v3

--- a/solution.py
+++ b/solution.py
@@ -157,16 +157,16 @@
 
 
 def _levels_kernel(x_at, cot_at, ka_at, kb_at, kc_at, kd_at,
-                   result_ref, input_grad_ref, early_out, late_out,
-                   x_ref, cot_ref, ka_ref, kb_ref, kc_ref, kd_ref,
+                   result_out, input_grad_out, early_out, late_out,
+                   result_ref, input_grad_ref, x_ref, cot_ref, ka_ref, kb_ref, kc_ref, kd_ref,
                    rows_ref, left_ref, right_ref, above_ref, below_ref, from_left_ref, from_right_ref,
                    up_corners, down_corners, above_corners, below_corners,
                    wa, wat, wb, wbt, wc, wct, wd, wdt, pool, spread,
                    x3, cot3, parts, cot_parts, cparts, hidden, slope_a, slope_b, coarse3, middle3,
                    coarse_out, joined3, grad_joined, grad_coarse3, grad_b3, grad_pool, up, grad_a3,
                    pad_a, pad_b, pad_c, pad_d, flat, acc, *rest):
-    load_sem, rim_send, rim_recv = rest[:3]
-    early_rest, late_rest = rest[3:23], rest[23:43]
+    load_sem, store_sem, rim_send, rim_recv = rest[:4]
+    early_rest, late_rest = rest[4:24], rest[24:44]
     row, col = lax.axis_index("rows"), lax.axis_index("cols")
     height, width = lax.axis_size("rows"), lax.axis_size("cols")
     top = (row == 0).astype(jnp.int32)
@@ -281,8 +281,8 @@
     push(down_corners, above_corners, (1, 0))
     for i in range(REACH, REACH + 16):
         unpack(i)
-    conv(wa, x3, parts, 7, 23, 4)
-    conv(wdt, cot3, cot_parts, 7, 23, 4)
+    conv(wa, x3, parts, 7, 23, 8)
+    conv(wdt, cot3, cot_parts, 7, 23, 8)
     for copy in rim[2:]:
         copy.wait_recv()
     for i in list(range(REACH)) + list(range(REACH + 16, 30)):
@@ -316,14 +316,14 @@
                 if with_slope:
                     slope_a[k - 2, :, 256 * s:256 * s + 256] = slope
         return step
-    _loop(0, 2, first(False))
-    _loop(2, 12, first(True))
-    _loop(12, 14, first(False))
+    _loop(0, 2, first(False), 2)
+    _loop(2, 12, first(True), 5)
+    _loop(12, 14, first(False), 2)
     clear(hidden, 3, 14)
 
     def pool_step(k):
         coarse3[k] = _taps((_dot(hidden[k], pool[...]) * 0.25).astype(BF).astype(F32))
-    _loop(0, 14, pool_step, 7)
+    _loop(0, 14, pool_step, 14)
 
     conv(wb, coarse3, cparts, 0, 14, 7)
 
@@ -331,23 +331,23 @@
         value, slope = _gelu_parts(gathered(cparts, k + 1, 128))
         middle3[k] = _taps(value * c_mask)
         slope_b[k] = slope
-    _loop(0, 12, second, 2)
+    _loop(0, 12, second, 6)
     clear(middle3, 2, 12)
 
     def third(k):
         cparts[k, 0:192] = _dot(wc[...], middle3[k])
-    _loop(0, 12, third, 6)
+    _loop(0, 12, third, 12)
 
     def third_sum(k):
         coarse_out[k] = (gathered(cparts, k + 1, 64) * c_mask).astype(BF)
-    _loop(0, 10, third_sum, 5)
+    _loop(0, 10, third_sum, 10)
     clear(coarse_out, 1, 10)
 
     def spread_step(source):
         def step(k):
             up[k] = _dot(source[k], spread[...])
         return step
-    _loop(0, 10, spread_step(coarse_out), 5)
+    _loop(0, 10, spread_step(coarse_out), 10)
 
     def join(k, s):
         both = hidden[k + 2, :, 256 * s:256 * s + 256].astype(F32) + up[k]
@@ -357,13 +357,13 @@
     def join_step(k):
         join(k, 0)
         join(k, 1)
-    _loop(1, 9, join_step, 2)
+    _loop(1, 9, join_step, 4)
     join(9, 0)
 
     def out_parts(weights, source):
         def step(i):
             parts[i, :, 0:128] = _dot(weights[...], source[i])
-        _loop(0, 18, step, 6)
+        _loop(0, 18, step, 9)
 
     def out_rows(ref):
         for h in range(16):
@@ -371,8 +371,6 @@
                 parts.at[:, :, pl.ds(0, 128)], h + 1, 64)
         ref[...] = flat[...].reshape(64, 16, 128).astype(BF)
 
-    out_parts(wd, joined3)
-    out_rows(result_ref)
 
     def stacked(pad, j):
         return jnp.concatenate([pad[j + 2], pad[j + 1], pad[j]], axis=0)
@@ -393,7 +391,7 @@
 
         def step(j):
             acc[0:192, 0:192] += _dot_t(pair(lambda i: stacked(pad, i), j), pair(window, j))
-        _loop(0, 9, step, 3)
+        _loop(0, 9, step, 9)
 
         def tap(t):
             if t > 8:
@@ -412,12 +410,12 @@
         for s in range(2):
             grad = gathered(cot_parts, 2 * k + 1 + s, 64) * f_mask
             grad_joined[k, :, 256 * s:256 * s + 256] = grad.astype(BF)
-    _loop(0, 14, back_first, 2)
+    _loop(0, 14, back_first, 7)
     clear(grad_joined, 3, 14)
 
     def back_pool(k):
         grad_coarse3[k] = _taps(_dot(grad_joined[k], pool[...]).astype(BF).astype(F32))
-    _loop(0, 14, back_pool, 7)
+    _loop(0, 14, back_pool, 14)
 
     framed(pad_c, 3, 8, lambda k: (grad_coarse3[k, 64:128, :].astype(F32) * own_c).astype(BF))
     acc[0:192, 0:384] = jnp.zeros((192, 384), F32)
@@ -425,7 +423,7 @@
     def c_step(j):
         acc[0:192, 0:384] += _dot_t(
             pair(lambda i: stacked(pad_c, i), j), pair(lambda i: middle3[i + 1], j))
-    _loop(0, 5, c_step, 1)
+    _loop(0, 5, c_step, 5)
     for a in range(3):
         for b in range(3):
             early_src[pl.ds(4 * (3 * a + b), 4)] = acc[
@@ -434,7 +432,7 @@
 
     def back_second(k):
         grad_b3[k] = _taps(slope_b[k] * gathered(cparts, k + 1, 128) * c_mask)
-    _loop(0, 12, back_second, 2)
+    _loop(0, 12, back_second, 6)
     clear(grad_b3, 2, 12)
 
     def b_own(k):
@@ -449,17 +447,17 @@
     def b_step(j):
         early_src[pl.ds(56, 36)] += _dot_t(
             pair(b_window, j), pair(lambda k: pad_b[k], j)).reshape(36, 16, 128)
-    _loop(0, 4, b_step, 2)
+    _loop(0, 4, b_step, 4)
     early.pair()
 
     def back_third(k):
         cparts[k, 0:192] = _dot(wbt[...], grad_b3[k])
-    _loop(0, 12, back_third, 6)
+    _loop(0, 12, back_third, 12)
 
     def back_third_sum(k):
         grad_pool[k] = gathered(cparts, k + 1, 64).astype(BF)
-    _loop(0, 10, back_third_sum, 5)
-    _loop(0, 10, spread_step(grad_pool), 5)
+    _loop(0, 10, back_third_sum, 10)
+    _loop(0, 10, spread_step(grad_pool), 10)
 
     def back_join(k, s):
         at = slice(256 * s, 256 * s + 256)
@@ -471,30 +469,42 @@
     def back_join_step(k):
         back_join(k, 0)
         back_join(k, 1)
-    _loop(1, 9, back_join_step, 2)
+    _loop(1, 9, back_join_step, 4)
     back_join(9, 0)
     clear(grad_a3, 1, 18)
     early.along_near()
     framed(pad_a, 1, 16, lambda h: grad_a3[h, 64:128, :])
     late_src[pl.ds(20, 12)] = jnp.zeros((12, 16, 128), F32)
     fine_weight_grad(pad_a, lambda i: x3[i + 6, :, 0:128], late_src, 0)
+    stores = []
+
+    def store(src, dst):
+        stores.append(pltpu.make_async_copy(src, dst, store_sem.at[len(stores)]))
+        stores[-1].start()
+
     late.pair()
     early.along_far()
+    out_parts(wd, joined3)
+    late.plane()
+    out_rows(result_ref)
+    store(result_ref, result_out)
     out_parts(wat, grad_a3)
-    late.plane()
-    out_rows(input_grad_ref)
     late.along_near()
     early.back_plane()
+    out_rows(input_grad_ref)
+    store(input_grad_ref, input_grad_out)
     late.along_far()
     early.back_pair()
     late.back_plane()
     early.finish()
-    early_out[...] = early.whole[...]
+    store(early.whole, early_out)
     late.back_pair()
     late.finish()
-    late_out[...] = late.whole[...]
+    store(late.whole, late_out)
     for copy in rim:
         copy.wait_send()
+    for copy in stores:
+        copy.wait()
 
 
 def _sum_scratch(tiles):
@@ -510,7 +520,7 @@
 
 def levels(level_input, cotangent, ka, kb, kc, kd):
     scratch = [
-        ((64, 16, 128), BF), ((64, 16, 128), BF),
+        ((64, 16, 128), BF), ((64, 16, 128), BF), ((64, 16, 128), BF), ((64, 16, 128), BF),
         ((9, 64, 64), BF), ((9, 64, 128), BF), ((9, 64, 128), BF), ((9, 64, 64), BF),
         ((16, 128, 128), BF), ((128, 128), BF), ((128, 128), BF),
         ((REACH, 128, 128), BF), ((REACH, 128, 128), BF), ((128, 128), BF), ((128, 128), BF),
@@ -534,9 +544,9 @@
         out_shape=(
             out((64, 16, 128), BF), out((64, 16, 128), BF), out((96, 16, 128), BF), out((32, 16, 128), BF)),
         in_specs=[pl.BlockSpec(memory_space=pltpu.HBM)] * 6,
-        out_specs=(VMEM,) * 4,
+        out_specs=(pl.BlockSpec(memory_space=pltpu.HBM),) * 4,
         scratch_shapes=[pltpu.VMEM(shape, dtype) for shape, dtype in scratch]
-        + [dma((6,)), dma((6,)), dma((6,))] + _sum_scratch(96) + _sum_scratch(32),
+        + [dma((6,)), dma((4,)), dma((6,)), dma((6,))] + _sum_scratch(96) + _sum_scratch(32),
         compiler_params=pltpu.CompilerParams(
             collective_id=0, has_side_effects=True, vmem_limit_bytes=60 * 1024 * 1024),
         cost_estimate=pl.CostEstimate(flops=2000000000, bytes_accessed=8000000, transcendentals=1000000),
@@ -564,7 +574,7 @@
             out((9, 64, 128), F32), out((9, 64, 128), F32), out((9, 64, 64), F32)),
         in_specs=[VMEM] * 4,
         out_specs=(VMEM,) * 6,
-        compiler_params=pltpu.CompilerParams(vmem_limit_bytes=8 * 1024 * 1024),
+        compiler_params=pltpu.CompilerParams(vmem_limit_bytes=60 * 1024 * 1024),
         cost_estimate=pl.CostEstimate(flops=1000000, bytes_accessed=2000000, transcendentals=0),
     )(result, input_grad, early, late)
 

time: 85 us -> 76.9 us (0.905)
  Pallas kernels: 80.3 us -> 76.1 us
  local copies, waits for them, and re-layouts: 3.79 us -> 0 us
    pallas_call x1, Pallas kernels: 79 us -> 73.6 us  [levels(): pl.pallas_call(_levels_kernel, out_shape=(out((64, 16, 128), BF), out((64...]
    unnamed x8 -> x0, local copies, waits for them, and re-layouts: 3.79 us -> none
    pallas_call x1, Pallas kernels: 1.25 us -> 2.44 us  [finish(): pl.pallas_call(functools.partial(_finish_kernel, fine_scale, coarse_scale...]
where the time goes in v4:
time: 76.9 us; the launch traced here: 76.7 us
  Pallas kernels  76.1 us (99%)
    pallas_call x1, Pallas kernels, levels(): pl.pallas_call(_levels_kernel, out_shape=(out((64, 16, 128), BF), out((64...  73.6 us
    pallas_call x1, Pallas kernels, finish(): pl.pallas_call(functools.partial(_finish_kernel, fine_scale, coarse_scale...  2.44 us

profile of v4, /device:TPU:1, one launch (start us, length us, event | category | flops | bytes accessed | tf_op | source)
XLA Modules:
  0.0 76.7 jit_solution(13368383427953092394)
XLA Ops:
  0.6 73.6 %shard_map.109 = (bf16[64,16,128]{2,1,0:T(8,128)(2,1)}, bf16[64,16,128]{2,1,0:T(8,128)(2,1)}, bf16[96,16,128]{2,1,0:T(8,128)(2,1)}, bf16[32,16,128]{2,1,0:T(8,128)(2,1)}) custom-call(bf16[64,16,128]{2,1,0:T(8,128)(2,1)} %x_at.1, bf16[64,16,128]{2,1,0:T(8,128)(2,1)} %cot_at.1, bf16[9,64,64]{2,1,0:T(8,128)(2,1)} %bitcast.28, bf16[9,64,128]{2,1,0:T(8,128)(2,1)} %bitcast.29, ...), custom_call_target="tpu_custom_call" | custom-call | flops 2000000000 | bytes 8000000 | tf_op jit(solution)/shard_map/pallas_call | solution.py:542
  74.3 2.4 %shard_map.110 = (bf16[64,16,128]{2,1,0:T(8,128)(2,1)}, bf16[64,16,128]{2,1,0:T(8,128)(2,1)}, f32[9,64,64]{2,1,0:T(8,128)}, f32[9,64,128]{2,1,0:T(8,128)}, f32[9,64,128]{2,1,0:T(8,128)}, /*index=5*/f32[9,64,64]{2,1,0:T(8,128)}) custom-call(bf16[64,16,128]{2,1,0:T(8,128)(2,1)} %get-tuple-element.16.result_in, ...), custom_call_target="tpu_custom_call" | custom-call | flops 1000000 | bytes 2000000 | tf_op jit(solution)/shard_map/pallas_call | solution.py:570

commit v5 on v4

--- a/solution.py
+++ b/solution.py
@@ -384,7 +384,7 @@
 
         def step(h):
             pad[h + 2] = own(h + first)
-        _loop(0, count, step, 4)
+        _loop(0, count, step, 8)
 
     def fine_weight_grad(pad, window, src, first):
         acc[0:192, 0:192] = jnp.zeros((192, 192), F32)
@@ -463,7 +463,6 @@
         at = slice(256 * s, 256 * s + 256)
         grad = grad_joined[k + 2, :, at].astype(F32) + 0.25 * up[k]
         grad_a3[2 * k - 1 + s] = _taps(slope_a[k, :, at] * grad * f_mask)[:, 0:128]
-    early.plane()
     back_join(0, 1)
 
     def back_join_step(k):
@@ -472,7 +471,7 @@
     _loop(1, 9, back_join_step, 4)
     back_join(9, 0)
     clear(grad_a3, 1, 18)
-    early.along_near()
+    early.plane()
     framed(pad_a, 1, 16, lambda h: grad_a3[h, 64:128, :])
     late_src[pl.ds(20, 12)] = jnp.zeros((12, 16, 128), F32)
     fine_weight_grad(pad_a, lambda i: x3[i + 6, :, 0:128], late_src, 0)
@@ -483,22 +482,23 @@
         stores[-1].start()
 
     late.pair()
-    early.along_far()
     out_parts(wd, joined3)
     late.plane()
+    early.along_near()
     out_rows(result_ref)
     store(result_ref, result_out)
+    late.along_near()
     out_parts(wat, grad_a3)
-    late.along_near()
-    early.back_plane()
+    early.along_far()
+    late.along_far()
     out_rows(input_grad_ref)
     store(input_grad_ref, input_grad_out)
-    late.along_far()
+    early.back_plane()
+    late.back_plane()
     early.back_pair()
-    late.back_plane()
+    late.back_pair()
     early.finish()
     store(early.whole, early_out)
-    late.back_pair()
     late.finish()
     store(late.whole, late_out)
     for copy in rim:

time: 76.9 us -> 71.9 us (0.935)
  Pallas kernels: 76.1 us -> 71 us
    pallas_call x1, Pallas kernels: 73.6 us -> 68.6 us  [levels(): pl.pallas_call(_levels_kernel, out_shape=(out((64, 16, 128), BF), out((64...]
where the time goes in v5:
time: 71.9 us; the launch traced here: 71.7 us
  Pallas kernels  71 us (99%)
    pallas_call x1, Pallas kernels, levels(): pl.pallas_call(_levels_kernel, out_shape=(out((64, 16, 128), BF), out((64...  68.6 us
    pallas_call x1, Pallas kernels, finish(): pl.pallas_call(functools.partial(_finish_kernel, fine_scale, coarse_scale...  2.44 us

profile of v5, /device:TPU:1, one launch (start us, length us, event | category | flops | bytes accessed | tf_op | source)
XLA Modules:
  0.0 71.7 jit_solution(12973549395361488404)
XLA Ops:
  0.6 68.6 %shard_map.109 = (bf16[64,16,128]{2,1,0:T(8,128)(2,1)}, bf16[64,16,128]{2,1,0:T(8,128)(2,1)}, bf16[96,16,128]{2,1,0:T(8,128)(2,1)}, bf16[32,16,128]{2,1,0:T(8,128)(2,1)}) custom-call(bf16[64,16,128]{2,1,0:T(8,128)(2,1)} %x_at.1, bf16[64,16,128]{2,1,0:T(8,128)(2,1)} %cot_at.1, bf16[9,64,64]{2,1,0:T(8,128)(2,1)} %bitcast.28, bf16[9,64,128]{2,1,0:T(8,128)(2,1)} %bitcast.29, ...), custom_call_target="tpu_custom_call" | custom-call | flops 2000000000 | bytes 8000000 | tf_op jit(solution)/shard_map/pallas_call | solution.py:542
  69.3 2.4 %shard_map.110 = (bf16[64,16,128]{2,1,0:T(8,128)(2,1)}, bf16[64,16,128]{2,1,0:T(8,128)(2,1)}, f32[9,64,64]{2,1,0:T(8,128)}, f32[9,64,128]{2,1,0:T(8,128)}, f32[9,64,128]{2,1,0:T(8,128)}, /*index=5*/f32[9,64,64]{2,1,0:T(8,128)}) custom-call(bf16[64,16,128]{2,1,0:T(8,128)(2,1)} %get-tuple-element.16.result_in, ...), custom_call_target="tpu_custom_call" | custom-call | flops 1000000 | bytes 2000000 | tf_op jit(solution)/shard_map/pallas_call | solution.py:570
